TPU v7x, 256 devices: a whole 4x4x8 slice. The times are simulated.
256 devices in a mesh: dp: 32 (over y, x, core), chain: 8 (over z).
Axes of the slice: x: 4, y: 4, z: 8, core: 2. Of those that a mesh axis runs over, the one named last changes fastest.
Arguments:
- events: bfloat16 [32, 1024, 1024], P('dp', 'chain'), may hold values from -6 to 6
- destinations: int32 [32, 1024], P('dp', 'chain'), may hold values from 0 to 4095, as said below
- history_ids: int32 [32, 1024], P('dp'), may hold values from 0 to 2, never falling along the last dimension, each value on 1 to 768 neighbouring positions
- cotangent: bfloat16 [32, 1024, 1024], P('dp', 'chain'), may hold values from -6 to 6
- w_uvqk: bfloat16 [1024, 4096], replicated, may hold values from -0.1875 to 0.1875
- w_out: bfloat16 [1024, 1024], replicated, may hold values from -0.1875 to 0.1875
Outputs:
- layer_out: bfloat16 [32, 1024, 1024], P('dp', 'chain')
- event_grad: bfloat16 [32, 1024, 1024], P('dp', 'chain')
- weight_grad: float32 [1024, 1024], P('dp')
Inputs may be any that keep to these rules, and one draw needn't show every extreme that they name: destinations[d, c * 128 + i] = e * 128 + s moves that event to row c * 128 + s of group e; the map is one to one, and every device sends an equal share of its events to each dp index. history_ids never fall along a group; in each group one history holds exactly 768 events and the other histories share the rest.
All inputs are finite; a program needn't handle non-finite values.
Results may differ from a plain program's by a relative error of at most 0.025.
Values may be sent and summed in bfloat16 or wider, within the bound.
A program may use at most 128 MiB of HBM per device.

v0:
```python
import math

import jax
import jax.numpy as jnp
from jax import lax
from jax.sharding import PartitionSpec as P

HEADS = 8


epsilon = 1e-05


def passed_along(x, axis, by):
    peers = lax.axis_size(axis)
    pairs = [(i, i + by) for i in range(peers) if 0 <= i + by < peers]
    return lax.ppermute(x, axis, pairs)


def layer_norm(values):
    center = values - jnp.mean(values, axis=-1, keepdims=True)
    variance = jnp.mean(center * center, axis=-1, keepdims=True)
    return center * lax.rsqrt(variance + epsilon)


def norm_back(values, upstream):
    center = values - jnp.mean(values, axis=-1, keepdims=True)
    variance = jnp.mean(center * center, axis=-1, keepdims=True)
    inverse = lax.rsqrt(variance + epsilon)
    normed = center * inverse
    upstream_mean = jnp.mean(upstream, axis=-1, keepdims=True)
    product_mean = jnp.mean(upstream * normed, axis=-1, keepdims=True)
    return inverse * (upstream - upstream_mean - normed * product_mean)


def silu_slope(values):
    sigmoid = jax.nn.sigmoid(values)
    return sigmoid * (1.0 + values * (1.0 - sigmoid))


def contract_last(left_side, right_side):
    return lax.dot_general(
        left_side, right_side, (((1,), (1,)), ((), ())), preferred_element_type=jnp.float32
    )


def on_device(events, destinations, history_ids, cotangent, w_uvqk, w_out):
    row_count = events.shape[1]
    model_width = events.shape[2]
    dp_size = lax.axis_size("dp")
    chain_size = lax.axis_size("chain")
    per_peer = row_count // dp_size
    target = destinations[0] // row_count
    slot_local = destinations[0] % row_count
    row_order = jnp.arange(row_count, dtype=jnp.int32)
    earlier = (target[None, :] == target[:, None]) & (row_order[None, :] < row_order[:, None])
    sent_at = target * per_peer + jnp.sum(earlier.astype(jnp.int32), axis=1)
    outgoing = jnp.zeros_like(events[0]).at[sent_at].set(events[0])
    outgoing_slots = jnp.zeros((row_count,), jnp.int32).at[sent_at].set(slot_local)
    arrived, arrived_slots = (
        lax.all_to_all(
            outgoing.reshape(dp_size, per_peer, model_width),
            "dp",
            split_axis=0,
            concat_axis=0,
            tiled=True,
        ),
        lax.all_to_all(
            outgoing_slots.reshape(dp_size, per_peer), "dp", split_axis=0, concat_axis=0, tiled=True
        ),
    )
    arrived_slots = arrived_slots.reshape(row_count)
    grouped = (
        jnp.zeros((row_count, model_width), events.dtype)
        .at[arrived_slots]
        .set(arrived.reshape(row_count, model_width))
    )
    head_dim = model_width // HEADS
    alpha = head_dim ** (-0.5)
    residual = grouped.astype(jnp.float32)
    normed = layer_norm(residual).astype(jnp.bfloat16)
    pre_act = jnp.dot(normed, w_uvqk, preferred_element_type=jnp.float32)
    projected = jax.nn.silu(pre_act).astype(jnp.bfloat16)
    gating = projected[:, :model_width].astype(jnp.float32)
    query_flat = projected[:, 2 * model_width : 3 * model_width]
    queries = query_flat.reshape(row_count, HEADS, head_dim)
    panel = jnp.concatenate(
        [projected[:, 3 * model_width :], projected[:, model_width : 2 * model_width]], axis=1
    )
    chain_at = lax.axis_index("chain")
    arrived_panels = [panel]
    moving = panel
    for hop_number in range(1, chain_size):
        moving = passed_along(moving, "chain", 1)
        arrived_panels.append(moving)
    stacked = jnp.stack(arrived_panels[::-1], axis=0)
    panels_all = jnp.roll(stacked, chain_at - (chain_size - 1), axis=0).reshape(
        chain_size * row_count, 2 * model_width
    )
    token_total = panels_all.shape[0]
    keys_all = panels_all[:, :model_width].reshape(token_total, HEADS, head_dim)
    values_all = panels_all[:, model_width:].reshape(token_total, HEADS, head_dim)
    history = history_ids[0]
    query_pos = chain_at * row_count + row_order
    key_pos = jnp.arange(token_total, dtype=jnp.int32)
    query_history = lax.dynamic_slice_in_dim(history, chain_at * row_count, row_count)
    visible = (query_history[:, None] == history[None, :]) & (
        key_pos[None, :] <= query_pos[:, None]
    )
    scores = (
        jnp.einsum("qhd,khd->hqk", queries, keys_all, preferred_element_type=jnp.float32) * alpha
    )
    attention = jnp.where(visible[None], jax.nn.silu(scores), 0.0).astype(jnp.bfloat16)
    mixed = jnp.einsum(
        "hqk,khd->qhd", attention, values_all, preferred_element_type=jnp.float32
    ).reshape(row_count, model_width)
    mixed_norm = layer_norm(mixed)
    gated = (mixed_norm * gating).astype(jnp.bfloat16)
    layer_out = (residual + jnp.dot(gated, w_out, preferred_element_type=jnp.float32)).astype(
        jnp.bfloat16
    )
    upstream = cotangent[0]
    gated_grad = contract_last(upstream, w_out)
    gating_grad = gated_grad * mixed_norm
    mixed_grad = norm_back(mixed, gated_grad * gating).astype(jnp.bfloat16)
    mixed_heads = mixed_grad.reshape(row_count, HEADS, head_dim)
    attention_grad = jnp.einsum(
        "qhd,khd->hqk", mixed_heads, values_all, preferred_element_type=jnp.float32
    )
    score_grad = jnp.where(visible[None], attention_grad * silu_slope(scores) * alpha, 0.0).astype(
        jnp.bfloat16
    )
    query_grad = jnp.einsum(
        "hqk,khd->qhd", score_grad, keys_all, preferred_element_type=jnp.float32
    ).reshape(row_count, model_width)
    key_part = jnp.einsum(
        "hqk,qhd->khd", score_grad, queries, preferred_element_type=jnp.float32
    ).reshape(row_count * lax.axis_size("chain"), model_width)
    value_part = jnp.einsum(
        "hqk,qhd->khd", attention, mixed_heads, preferred_element_type=jnp.float32
    ).reshape(row_count * lax.axis_size("chain"), model_width)
    panel_grad = lax.psum_scatter(
        jnp.concatenate([key_part, value_part], axis=1).astype(jnp.bfloat16),
        "chain",
        scatter_dimension=0,
        tiled=True,
    ).astype(jnp.float32)
    key_grad = panel_grad[:, :model_width]
    value_grad = panel_grad[:, model_width:]
    pre_grad = (
        jnp.concatenate([gating_grad, value_grad, query_grad, key_grad], axis=1)
        * silu_slope(pre_act)
    ).astype(jnp.bfloat16)
    normed_grad = contract_last(pre_grad, w_uvqk)
    input_grad = (upstream.astype(jnp.float32) + norm_back(residual, normed_grad)).astype(
        jnp.bfloat16
    )
    returning = input_grad[arrived_slots].reshape(dp_size, per_peer, model_width)
    returned = lax.all_to_all(returning, "dp", split_axis=0, concat_axis=0, tiled=True).reshape(
        row_count, model_width
    )
    event_grad = returned[sent_at]
    grad_scale = 1.0 / math.sqrt(row_count * dp_size * chain_size)
    partial_grad = lax.psum_scatter(
        (
            lax.dot_general(
                gated, upstream, (((0,), (0,)), ((), ())), preferred_element_type=jnp.float32
            )
            * grad_scale
        ).astype(jnp.bfloat16),
        "dp",
        scatter_dimension=0,
        tiled=True,
    )
    weight_grad = lax.psum(partial_grad, "chain").astype(jnp.float32)
    return (layer_out[None], event_grad[None], weight_grad)


def solution(mesh):
    return jax.shard_map(
        on_device,
        mesh=mesh,
        in_specs=(
            P("dp", "chain", None),
            P("dp", "chain"),
            P("dp", None),
            P("dp", "chain", None),
            P(),
            P(),
        ),
        out_specs=(P("dp", "chain", None), P("dp", "chain", None), P("dp", None)),
        check_vma=False,
    )
```

profile of v0, /device:TPU:1, one launch (start us, length us, event | category | flops | bytes accessed | tf_op | source)
XLA Modules:
  0.0 433.0 jit_solution(18177285593555559438)
XLA Ops:
  11.2 8.6 %all-to-all-start = ((s32[32,1,4]{2,1,0:T(1,128)}), s32[32,1,4]{2,1,0:T(1,128)S(1)}, u32[]{:S(2)}, u32[]{:S(2)}) async-start(s32[32,1,4]{2,1,0:T(1,128)} %bitcast.5), calls=%async_computation | async-start | bytes 32768 | tf_op jit(solution)/shard_map/all_to_all | solution.py:68
  22.2 4.4 %all-to-all-done = s32[32,1,4]{2,1,0:T(1,128)S(1)} async-done(((s32[32,1,4]{2,1,0:T(1,128)}), s32[32,1,4]{2,1,0:T(1,128)S(1)}, u32[]{:S(2)}, u32[]{:S(2)}) %all-to-all-start) | async-done | bytes 544 | tf_op jit(solution)/shard_map/all_to_all | solution.py:68
  26.7 4.2 all-to-all-start.1
  32.2 7.6 %all-to-all-done.1 = bf16[32,4,1024]{2,1,0:T(4,128)(2,1)S(1)} async-done(((bf16[32,4,1024]{2,1,0:T(4,128)(2,1)}), bf16[32,4,1024]{2,1,0:T(4,128)(2,1)S(1)}, u32[]{:S(2)}, u32[]{:S(2)}) %all-to-all-start.1) | async-done | bytes 262176 | tf_op jit(solution)/shard_map/all_to_all | solution.py:61
  41.5 6.1 %multiply_convert_fusion.1 = (bf16[128,4096]{1,0:T(8,128)(2,1)S(1)}, f32[128,4096]{1,0:T(8,128)}) fusion(bf16[1024,4096]{1,0:T(8,128)(2,1)} %param.10, bf16[128,1024]{1,0:T(8,128)(2,1)S(1)} %scatter_custom_fusion.2, f32[128]{0:T(128)S(1)} %add_rsqrt_fusion.1, f32[128]{0:T(128)S(1)} %broadcast_multiply_fusion.5), kind=kOutput, calls=%fused_computation.12 | convolution fusion | flops 1076887552 | bytes 11797504 | tf_op jit(solution)/shard_map/dot_general | solution.py:82
  52.1 11.0 %collective-permute-done = bf16[128,2048]{1,0:T(8,128)(2,1)S(1)} collective-permute-done((bf16[128,2048]{1,0:T(8,128)(2,1)S(1)}, bf16[128,2048]{1,0:T(8,128)(2,1)S(1)}, u32[]{:S(2)}, u32[]{:S(2)}) %collective-permute-start) | collective-permute-done | bytes 524320 | tf_op jit(solution)/shard_map/ppermute | solution.py:17
  63.2 4.1 collective-permute-start.1
  67.3 10.1 %collective-permute-done.1 = bf16[128,2048]{1,0:T(8,128)(2,1)S(1)} collective-permute-done((bf16[128,2048]{1,0:T(8,128)(2,1)S(1)}, bf16[128,2048]{1,0:T(8,128)(2,1)S(1)}, u32[]{:S(2)}, u32[]{:S(2)}) %collective-permute-start.1) | collective-permute-done | bytes 524320 | tf_op jit(solution)/shard_map/ppermute | solution.py:17
  78.2 4.1 collective-permute-start.2
  82.3 9.2 %collective-permute-done.2 = bf16[128,2048]{1,0:T(8,128)(2,1)S(1)} collective-permute-done((bf16[128,2048]{1,0:T(8,128)(2,1)S(1)}, bf16[128,2048]{1,0:T(8,128)(2,1)S(1)}, u32[]{:S(2)}, u32[]{:S(2)}) %collective-permute-start.2) | collective-permute-done | bytes 524320 | tf_op jit(solution)/shard_map/ppermute | solution.py:17
  96.5 8.3 %collective-permute-done.3 = bf16[128,2048]{1,0:T(8,128)(2,1)S(1)} collective-permute-done((bf16[128,2048]{1,0:T(8,128)(2,1)S(1)}, bf16[128,2048]{1,0:T(8,128)(2,1)S(1)}, u32[]{:S(2)}, u32[]{:S(2)}) %collective-permute-start.3) | collective-permute-done | bytes 524320 | tf_op jit(solution)/shard_map/ppermute | solution.py:17
  105.6 4.9 %collective-permute-start.4 = (bf16[128,2048]{1,0:T(8,128)(2,1)S(1)}, bf16[128,2048]{1,0:T(8,128)(2,1)S(1)}, u32[]{:S(2)}, u32[]{:S(2)}) collective-permute-start(bf16[128,2048]{1,0:T(8,128)(2,1)S(1)} %collective-permute-done.3), channel_id=1, source_target_pairs={{0,1},{1,2},{2,3},{3,4},{4,5},{5,6},{6,7},{8,9},{9,10},{10,11},{11... | collective-permute-start | bytes 1572872 | tf_op jit(solution)/shard_map/ppermute | solution.py:17
  110.4 7.4 %collective-permute-done.4 = bf16[128,2048]{1,0:T(8,128)(2,1)S(1)} collective-permute-done((bf16[128,2048]{1,0:T(8,128)(2,1)S(1)}, bf16[128,2048]{1,0:T(8,128)(2,1)S(1)}, u32[]{:S(2)}, u32[]{:S(2)}) %collective-permute-start.4) | collective-permute-done | bytes 524320 | tf_op jit(solution)/shard_map/ppermute | solution.py:17
  118.6 6.1 %collective-permute-start.5 = (bf16[128,2048]{1,0:T(8,128)(2,1)S(1)}, bf16[128,2048]{1,0:T(8,128)(2,1)}, u32[]{:S(2)}, u32[]{:S(2)}) collective-permute-start(bf16[128,2048]{1,0:T(8,128)(2,1)S(1)} %collective-permute-done.4), channel_id=1, source_target_pairs={{0,1},{1,2},{2,3},{3,4},{4,5},{5,6},{6,7},{8,9},{9,10},{10,11},{11... | collective-permute-start | bytes 1572872 | tf_op jit(solution)/shard_map/ppermute | solution.py:17
  124.7 5.7 %collective-permute-done.5 = bf16[128,2048]{1,0:T(8,128)(2,1)} collective-permute-done((bf16[128,2048]{1,0:T(8,128)(2,1)S(1)}, bf16[128,2048]{1,0:T(8,128)(2,1)}, u32[]{:S(2)}, u32[]{:S(2)}) %collective-permute-start.5) | collective-permute-done | bytes 524320 | tf_op jit(solution)/shard_map/ppermute | solution.py:17
  130.4 6.1 %collective-permute-start.6 = (bf16[128,2048]{1,0:T(8,128)(2,1)}, bf16[128,2048]{1,0:T(8,128)(2,1)}, u32[]{:S(2)}, u32[]{:S(2)}) collective-permute-start(bf16[128,2048]{1,0:T(8,128)(2,1)} %collective-permute-done.5), channel_id=1, source_target_pairs={{0,1},{1,2},{2,3},{3,4},{4,5},{5,6},{6,7},{8,9},{9,10},{10,11},{11... | collective-permute-start | bytes 1572872 | tf_op jit(solution)/shard_map/ppermute | solution.py:17
  160.2 5.5 %select_convert_fusion.1 = (bf16[8,128,1024]{2,1,0:T(8,128)(2,1)S(1)}, f32[8,128,1024]{2,1,0:T(8,128)}) fusion(pred[128,1024]{1,0:T(8,128)(4,1)S(1)} %fusion.20, bf16[128,8,128]{0,2,1:T(8,128)(2,1)S(1)} %bitcast.126, bf16[1024,8,128]{0,2,1:T(8,128)(2,1)} %bitcast.120), kind=kOutput, calls=%fused_computation.8 | convolution fusion | flops 275775488 | bytes 8781824 | tf_op jit(solution)/shard_map/qhd,khd->hqk/dot_general | solution.py:111
  177.5 4.1 select_convert_fusion
  193.0 4.8 %pad_maximum_fusion = bf16[1024,2048]{1,0:T(8,128)(2,1)} fusion(bf16[1024,1024]{1,0:T(8,128)(2,1)} %copy.61, bf16[1024,1024]{1,0:T(8,128)(2,1)} %copy.60), kind=kLoop, calls=%fused_computation.5 | loop fusion | flops 8388608 | bytes 8388608 | tf_op jit(solution)/shard_map/concatenate | solution.py:143
  206.0 60.2 %reduce-scatter.3.cloned.1.call-done = bf16[128,2048]{1,0:T(8,128)(2,1)} async-done(((bf16[1024,2048]{1,0:T(8,128)(2,1)}), bf16[128,2048]{1,0:T(8,128)(2,1)}) %reduce-scatter.3.cloned.1.call-update) | async-done | bytes 524304 | tf_op jit(solution)/shard_map/reduce_scatter | solution.py:142
  267.4 7.4 %fusion.43 = (f32[128]{0:T(128)S(1)}, f32[128]{0:T(128)S(1)}, f32[128,1024]{1,0:T(8,128)S(1)}) fusion(f32[128]{0:T(128)S(1)} %add_rsqrt_fusion.1, f32[128]{0:T(128)S(1)} %broadcast_multiply_fusion.5, bf16[128,1024]{1,0:T(8,128)(2,1)S(1)} %scatter_custom_fusion.2, bf16[1024,4096]{1,0:T(8,128)(2,1)} %param.10, f32[128,1024]{1,0:T(8,128)S(1)} %get-tuple-element.16, ...), kind=kOutput, calls=%fused_computation.116 | convolution fusion | flops 1080819456 | bytes 13371392 | tf_op jit(solution)/shard_map/dot_general | solution.py:42
  276.8 7.5 %all-to-all-start.2 = ((bf16[32,4,1024]{2,1,0:T(4,128)(2,1)}), bf16[32,4,1024]{2,1,0:T(4,128)(2,1)S(1)}, u32[]{:S(2)}, u32[]{:S(2)}) async-start(bf16[32,4,1024]{2,1,0:T(4,128)(2,1)} %reshape.294), calls=%async_computation.3 | async-start | bytes 524288 | tf_op jit(solution)/shard_map/all_to_all | solution.py:159
  284.3 69.2 %reduce-scatter.5.cloned.1.call-done = bf16[32,1024]{1,0:T(8,128)(2,1)} async-done(((bf16[1024,1024]{1,0:T(8,128)(2,1)}), bf16[32,1024]{1,0:T(8,128)(2,1)}) %reduce-scatter.5.cloned.1.call-update) | async-done | bytes 65552 | tf_op jit(solution)/shard_map/reduce_scatter | solution.py:164
  354.7 68.7 %all-reduce.2.cloned.1.call-done = bf16[32,1024]{1,0:T(8,128)(2,1)} async-done(((bf16[32,1024]{1,0:T(8,128)(2,1)}), bf16[32,1024]{1,0:T(8,128)(2,1)}) %all-reduce.2.cloned.1.call-update) | async-done | bytes 65552 | tf_op jit(solution)/shard_map/psum | solution.py:175
  (124 shorter events, 83.6 us)
Async XLA Ops:
  7.2 161.0 %copy-start = (bf16[1024,1024]{1,0:T(8,128)(2,1)S(1)}, bf16[1024,1024]{1,0:T(8,128)(2,1)}, u32[]{:S(2)}) copy-start(bf16[1024,1024]{1,0:T(8,128)(2,1)} %param.11) | copy-start | bytes 6291460
  9.5 21.4 %copy-start.17 = (s32[128]{0:T(128)}, s32[128]{0:T(128)S(1)}, u32[]{:S(2)}) copy-start(s32[128]{0:T(128)S(1)} %fusion.36) | copy-start | bytes 1540
  11.2 15.5 %all-to-all-start = ((s32[32,1,4]{2,1,0:T(1,128)}), s32[32,1,4]{2,1,0:T(1,128)S(1)}, u32[]{:S(2)}, u32[]{:S(2)}) async-start(s32[32,1,4]{2,1,0:T(1,128)} %bitcast.5), calls=%async_computation | async-start | bytes 32768 | tf_op jit(solution)/shard_map/all_to_all | solution.py:68
  26.7 13.2 %all-to-all-start.1 = ((bf16[32,4,1024]{2,1,0:T(4,128)(2,1)}), bf16[32,4,1024]{2,1,0:T(4,128)(2,1)S(1)}, u32[]{:S(2)}, u32[]{:S(2)}) async-start(bf16[32,4,1024]{2,1,0:T(4,128)(2,1)} %reshape.283), calls=%async_computation.1 | async-start | bytes 524288 | tf_op jit(solution)/shard_map/all_to_all | solution.py:61
  30.9 235.4 %reduce-scatter.3.cloned.1.call-start = ((), (), s32[]{:S(2)}) async-start(), calls=%async_computation.5 | async-start | bytes 4718592 | tf_op jit(solution)/shard_map/reduce_scatter | solution.py:142
  32.2 15.4 %copy-start.19 = (s32[128]{0:T(128)}, s32[128]{0:T(128)S(1)}, u32[]{:S(2)}) copy-start(s32[128]{0:T(128)S(1)} %fusion.37) | copy-start | bytes 1540
  41.5 95.0 %copy-start.16 = (s32[1,1024]{1,0:T(1,128)S(1)}, s32[1,1024]{1,0:T(1,128)}, u32[]{:S(2)}) copy-start(s32[1,1024]{1,0:T(1,128)} %param.8) | copy-start | bytes 12292
  47.6 82.7 %copy-start.14 = (bf16[128,4096]{1,0:T(8,128)(2,1)}, bf16[128,4096]{1,0:T(8,128)(2,1)S(1)}, u32[]{:S(2)}) copy-start(bf16[128,4096]{1,0:T(8,128)(2,1)S(1)} %get-tuple-element.19) | copy-start | bytes 3145732
  48.5 14.6 %collective-permute-start = (bf16[128,2048]{1,0:T(8,128)(2,1)S(1)}, bf16[128,2048]{1,0:T(8,128)(2,1)S(1)}, u32[]{:S(2)}, u32[]{:S(2)}) collective-permute-start(bf16[128,2048]{1,0:T(8,128)(2,1)S(1)} %pad_maximum_fusion.1), channel_id=1, source_target_pairs={{0,1},{1,2},{2,3},{3,4},{4,5},{5,6},{6,7},{8,9},{9,10},{10,11},{11... | collective-permute-start | bytes 1572872 | tf_op jit(solution)/shard_map/ppermute | solution.py:17
  63.2 14.3 %collective-permute-start.1 = (bf16[128,2048]{1,0:T(8,128)(2,1)S(1)}, bf16[128,2048]{1,0:T(8,128)(2,1)S(1)}, u32[]{:S(2)}, u32[]{:S(2)}) collective-permute-start(bf16[128,2048]{1,0:T(8,128)(2,1)S(1)} %collective-permute-done), channel_id=1, source_target_pairs={{0,1},{1,2},{2,3},{3,4},{4,5},{5,6},{6,7},{8,9},{9,10},{10,11},{11... | collective-permute-start | bytes 1572872 | tf_op jit(solution)/shard_map/ppermute | solution.py:17
  78.2 13.3 %collective-permute-start.2 = (bf16[128,2048]{1,0:T(8,128)(2,1)S(1)}, bf16[128,2048]{1,0:T(8,128)(2,1)S(1)}, u32[]{:S(2)}, u32[]{:S(2)}) collective-permute-start(bf16[128,2048]{1,0:T(8,128)(2,1)S(1)} %collective-permute-done.1), channel_id=1, source_target_pairs={{0,1},{1,2},{2,3},{3,4},{4,5},{5,6},{6,7},{8,9},{9,10},{10,11},{11... | collective-permute-start | bytes 1572872 | tf_op jit(solution)/shard_map/ppermute | solution.py:17
  92.4 12.4 %collective-permute-start.3 = (bf16[128,2048]{1,0:T(8,128)(2,1)S(1)}, bf16[128,2048]{1,0:T(8,128)(2,1)S(1)}, u32[]{:S(2)}, u32[]{:S(2)}) collective-permute-start(bf16[128,2048]{1,0:T(8,128)(2,1)S(1)} %collective-permute-done.2), channel_id=1, source_target_pairs={{0,1},{1,2},{2,3},{3,4},{4,5},{5,6},{6,7},{8,9},{9,10},{10,11},{11... | collective-permute-start | bytes 1572872 | tf_op jit(solution)/shard_map/ppermute | solution.py:17
  105.6 12.2 %collective-permute-start.4 = (bf16[128,2048]{1,0:T(8,128)(2,1)S(1)}, bf16[128,2048]{1,0:T(8,128)(2,1)S(1)}, u32[]{:S(2)}, u32[]{:S(2)}) collective-permute-start(bf16[128,2048]{1,0:T(8,128)(2,1)S(1)} %collective-permute-done.3), channel_id=1, source_target_pairs={{0,1},{1,2},{2,3},{3,4},{4,5},{5,6},{6,7},{8,9},{9,10},{10,11},{11... | collective-permute-start | bytes 1572872 | tf_op jit(solution)/shard_map/ppermute | solution.py:17
  118.6 11.8 %collective-permute-start.5 = (bf16[128,2048]{1,0:T(8,128)(2,1)S(1)}, bf16[128,2048]{1,0:T(8,128)(2,1)}, u32[]{:S(2)}, u32[]{:S(2)}) collective-permute-start(bf16[128,2048]{1,0:T(8,128)(2,1)S(1)} %collective-permute-done.4), channel_id=1, source_target_pairs={{0,1},{1,2},{2,3},{3,4},{4,5},{5,6},{6,7},{8,9},{9,10},{10,11},{11... | collective-permute-start | bytes 1572872 | tf_op jit(solution)/shard_map/ppermute | solution.py:17
  130.4 11.7 %collective-permute-start.6 = (bf16[128,2048]{1,0:T(8,128)(2,1)}, bf16[128,2048]{1,0:T(8,128)(2,1)}, u32[]{:S(2)}, u32[]{:S(2)}) collective-permute-start(bf16[128,2048]{1,0:T(8,128)(2,1)} %collective-permute-done.5), channel_id=1, source_target_pairs={{0,1},{1,2},{2,3},{3,4},{4,5},{5,6},{6,7},{8,9},{9,10},{10,11},{11... | collective-permute-start | bytes 1572872 | tf_op jit(solution)/shard_map/ppermute | solution.py:17
  138.5 8.1 %copy-start.9 = (bf16[128,2048]{1,0:T(8,128)(2,1)S(1)}, bf16[128,2048]{1,0:T(8,128)(2,1)}, u32[]{:S(2)}) copy-start(bf16[128,2048]{1,0:T(8,128)(2,1)} %copy-done.8) | copy-start | bytes 1572868
  138.5 8.1 %copy-start.7 = (bf16[128,2048]{1,0:T(8,128)(2,1)S(1)}, bf16[128,2048]{1,0:T(8,128)(2,1)}, u32[]{:S(2)}) copy-start(bf16[128,2048]{1,0:T(8,128)(2,1)} %copy-done.6) | copy-start | bytes 1572868
  144.3 4.7 %copy-start.13 = (bf16[128,2048]{1,0:T(8,128)(2,1)S(1)}, bf16[128,2048]{1,0:T(8,128)(2,1)}, u32[]{:S(2)}) copy-start(bf16[128,2048]{1,0:T(8,128)(2,1)} %copy-done.12) | copy-start | bytes 1572868
  152.3 7.9 %copy-start.15 = (bf16[128,1024]{0,1:T(8,128)(2,1)S(1)}, bf16[128,1024]{0,1:T(8,128)(2,1)}, u32[]{:S(2)}) copy-start(bf16[128,1024]{0,1:T(8,128)(2,1)} %copy.63) | copy-start | bytes 786436
  160.2 5.5 %copy-start.1 = (bf16[1024,1024]{0,1:T(8,128)(2,1)S(1)}, bf16[1024,1024]{0,1:T(8,128)(2,1)}, u32[]{:S(2)}) copy-start(bf16[1024,1024]{0,1:T(8,128)(2,1)} %copy.45) | copy-start | bytes 6291460
  197.8 155.7 %reduce-scatter.5.cloned.1.call-start = ((), (), s32[]{:S(2)}) async-start(), calls=%async_computation.6 | async-start | bytes 2162688 | tf_op jit(solution)/shard_map/reduce_scatter | solution.py:164
  274.8 9.5 %copy-start.18 = (s32[128]{0:T(128)S(1)}, s32[128]{0:T(128)}, u32[]{:S(2)}) copy-start(s32[128]{0:T(128)} %copy-done.17) | copy-start | bytes 1540
  276.8 148.1 %all-to-all-start.2 = ((bf16[32,4,1024]{2,1,0:T(4,128)(2,1)}), bf16[32,4,1024]{2,1,0:T(4,128)(2,1)S(1)}, u32[]{:S(2)}, u32[]{:S(2)}) async-start(bf16[32,4,1024]{2,1,0:T(4,128)(2,1)} %reshape.294), calls=%async_computation.3 | async-start | bytes 524288 | tf_op jit(solution)/shard_map/all_to_all | solution.py:159
  284.2 139.1 %all-reduce.2.cloned.1.call-start = ((), (), s32[]{:S(2)}) async-start(), calls=%async_computation.7 | async-start | bytes 131072 | tf_op jit(solution)/shard_map/psum | solution.py:175
  (10 other events, 18.3 us)
Sparse Core Ops, SparseCore 0:
  197.9 68.2 reduce-scatter.2
  270.1 83.3 reduce-scatter.4
  355.8 67.5 all-reduce.1
where the time goes:
time: 438 us; the launch traced here: 433 us
  waiting for transfers between devices  265 us (61%)
  starting transfers between devices  53.6 us (12%)
  local copies, waits for them, and re-layouts  48.3 us (11%)
  matrix products  38.8 us (9%)
  between operations  14.2 us (3%)
  other arithmetic  12.7 us (3%)
    reduce_scatter x1, waiting for transfers between devices, on_device(): lax.psum_scatter((lax.dot_general(gated, upstream, (((0,), (0,)), ((), ()...  69.2 us
    psum x1, waiting for transfers between devices, on_device(): weight_grad = lax.psum(partial_grad, 'chain').astype(jnp.float32)  68.7 us
    reduce_scatter x1, waiting for transfers between devices, on_device(): lax.psum_scatter(jnp.concatenate([key_part, value_part], axis=1).astype(j...  60.2 us
    ppermute x7, waiting for transfers between devices, passed_along(): return lax.ppermute(x, axis, pairs)  55.3 us
    ppermute x7, starting transfers between devices, passed_along(): return lax.ppermute(x, axis, pairs)  33 us
    unnamed x56, local copies, waits for them, and re-layouts  12.1 us
    dot_general x2, matrix products, contract_last(): lax.dot_general(left_side, right_side, (((1,), (1,)), ((), ())), preferre...  9.46 us
  transfers between devices with their start and end apart: 13, of which 12 were waited for; matrix products, arithmetic and copies ran while one was open for 6% of the time, Pallas kernels for 0%

commit v1 on v0

v1 whole, which is shorter than its diff:
```python
import functools
import math

import jax
import jax.numpy as jnp
from jax import lax
from jax.experimental import pallas as pl
from jax.experimental.pallas import tpu as pltpu
from jax.sharding import PartitionSpec as P

HEADS = 8
MESH = pl.DeviceIdType.MESH
BF = jnp.bfloat16
F32 = jnp.float32
I32 = jnp.int32
epsilon = 1e-05


def dot(a, b):
    return lax.dot_general(a, b, (((1,), (0,)), ((), ())), preferred_element_type=F32)


def dot_nt(a, b):
    return lax.dot_general(a, b, (((1,), (1,)), ((), ())), preferred_element_type=F32)


def dot_tn(a, b):
    return lax.dot_general(a, b, (((0,), (0,)), ((), ())), preferred_element_type=F32)


def sigmoid(v):
    return 0.5 * jnp.tanh(0.5 * v) + 0.5


def iota(shape, dim):
    return lax.broadcasted_iota(I32, shape, dim)


def mean(v):
    return jnp.mean(v, axis=-1, keepdims=True)


def one_hot(mask):
    return jnp.where(mask, 1.0, 0.0).astype(BF)


def kernel(
    n_dp,
    n_chain,
    ev_ref,
    dest_ref,
    hist_ref,
    ct_ref,
    wu_hbm,
    wo_hbm,
    layer_out_ref,
    event_grad_ref,
    weight_grad_ref,
    wu,
    wo,
    ev_send,
    ev_recv,
    residual_ref,
    normed_ref,
    pre_ref,
    gating_ref,
    gated_grad_ref,
    qkv_send,
    qkv,
    hist_col,
    att,
    slope,
    sgrad,
    mix_send,
    mix_recv,
    mg_send,
    mg,
    gated_ref,
    wg_send,
    wg_recv,
    d_send,
    d_recv,
    pg_ref,
    ng_ref,
    part_send,
    part_recv,
    full_send,
    full_recv,
    ret_send,
    ret_recv,
    load_sem,
    local_sem,
    ev_sems,
    wg_sems,
    ret_sems,
    qkv_ss,
    qkv_rs,
    mix_ss,
    mix_rs,
    mg_ss,
    mg_rs,
    d_ss,
    d_rs,
    part_ss,
    part_rs,
    full_ss,
    full_rs,
):
    rows, width = ev_ref.shape
    head = width // HEADS
    tokens = rows * n_chain
    per_peer = rows // n_dp
    fold = max(1, 16 // per_peer)
    block = per_peer * fold
    total = rows * fold
    cols = width // fold
    alpha = head ** (-0.5)
    share = width // n_dp
    e = lax.axis_index("dp")
    c = lax.axis_index("chain")

    load_wu = pltpu.make_async_copy(wu_hbm, wu, load_sem.at[0])
    load_wo = pltpu.make_async_copy(wo_hbm, wo, load_sem.at[1])
    load_wu.start()
    load_wo.start()

    barrier = pltpu.get_barrier_semaphore()

    def greet(step, carry):
        pl.semaphore_signal(
            barrier, inc=1, device_id=(lax.rem(e + step, n_dp), c), device_id_type=MESH
        )
        return carry

    lax.fori_loop(1, n_dp, greet, 0)
    for step in range(1, n_chain):
        pl.semaphore_signal(
            barrier, inc=1, device_id=(e, lax.rem(c + step, n_chain)), device_id_type=MESH
        )

    ri = iota((rows, rows), 0)
    ci = iota((rows, rows), 1)
    eye = ri == ci
    d_row = jnp.broadcast_to(dest_ref[...], (rows, rows))
    d_col = jnp.sum(jnp.where(eye, d_row.astype(F32), 0.0), axis=1, keepdims=True)
    d_col = jnp.broadcast_to(d_col, (rows, rows)).astype(I32)
    t_row = d_row // rows
    t_col = d_col // rows
    same = t_row == t_col
    rank_row = jnp.sum(jnp.where(same & (ri < ci), 1.0, 0.0), axis=0, keepdims=True)
    rank_col = jnp.sum(jnp.where(same & (ci < ri), 1.0, 0.0), axis=1, keepdims=True)
    place_row = block * t_row[:1, :] + rank_row.astype(I32)
    place_col = block * t_col + jnp.broadcast_to(rank_col, (rows, rows)).astype(I32)
    slots = (d_col - t_col * rows).astype(F32).astype(BF)
    at_row = jnp.broadcast_to(place_row, (total, rows))
    at = iota((total, rows), 0)
    spread = jnp.concatenate(
        [one_hot(at == at_row + per_peer * q) for q in range(fold)], axis=1
    )
    packed = jnp.concatenate(
        [
            jnp.concatenate([ev_ref[:, cols * q : cols * (q + 1)], slots], axis=1)
            for q in range(fold)
        ],
        axis=0,
    )
    ev_send[...] = dot(spread, packed).astype(BF)
    own_ev = pl.ds(pl.multiple_of(e * block, block), block)
    ev_recv[own_ev, :] = ev_send[own_ev, :]

    pl.semaphore_wait(barrier, n_dp - 1 + n_chain - 1)

    def to_group(send, recv, sems, rows_each):
        here = pl.ds(pl.multiple_of(e * rows_each, rows_each), rows_each)

        def one(step, carry):
            peer = lax.rem(e + step, n_dp)
            there = pl.ds(pl.multiple_of(peer * rows_each, rows_each), rows_each)
            pltpu.make_async_remote_copy(
                src_ref=send.at[there],
                dst_ref=recv.at[here],
                send_sem=sems.at[0],
                recv_sem=sems.at[1],
                device_id=(peer, c),
                device_id_type=MESH,
            ).start()
            return carry

        return one

    def await_group(buffer, sem, rows_each):
        part = buffer.at[pl.ds(0, (n_dp - 1) * rows_each)]
        pltpu.make_async_copy(part, part, sem).wait()

    lax.fori_loop(1, n_dp, to_group(ev_send, ev_recv, ev_sems, block), 0)

    for b in range(n_chain):
        ids = jnp.broadcast_to(
            hist_ref[:, rows * b : rows * (b + 1)].astype(F32), (rows, rows)
        )
        hist_col[rows * b : rows * (b + 1), :] = jnp.broadcast_to(
            jnp.sum(jnp.where(eye, ids, 0.0), axis=1, keepdims=True), (rows, rows)
        )

    await_group(ev_recv, ev_sems.at[1], block)
    slot_col = ev_recv[:, cols : cols + rows].astype(F32).astype(I32)
    slot_row = jnp.concatenate(
        [
            jnp.sum(
                jnp.where(eye, slot_col[rows * b : rows * (b + 1), :], 0).astype(F32),
                axis=0,
                keepdims=True,
            )
            for b in range(fold)
        ],
        axis=1,
    ).astype(I32)
    slot_row = jnp.broadcast_to(slot_row, (rows, total))
    slot_here = slot_row == iota((rows, total), 0)
    quarter = lax.rem(iota((rows, total), 1), block) // per_peer
    arrived = ev_recv[:, :cols]
    residual = jnp.concatenate(
        [dot(one_hot(slot_here & (quarter == q)), arrived) for q in range(fold)], axis=1
    )
    residual_ref[...] = residual
    center = residual - mean(residual)
    inverse = lax.rsqrt(mean(center * center) + epsilon)
    normed_ref[...] = (center * inverse).astype(BF)

    def chain_copy(src, dst, send_sem, recv_sem, peer):
        away = lax.rem(peer - c + n_chain, n_chain)
        return pltpu.make_async_remote_copy(
            src_ref=src,
            dst_ref=dst,
            send_sem=send_sem.at[away],
            recv_sem=recv_sem.at[away],
            device_id=(e, peer),
            device_id_type=MESH,
        )

    mine = pl.ds(pl.multiple_of(c * rows, rows), rows)

    load_wu.wait()
    for turn in (2, 1, 3, 0):
        pair = lax.rem(c // 2 + turn, n_chain // 2)
        for slot, part in ((0, 2), (1, 3), (2, 1)):
            columns = pl.ds(pl.multiple_of(part * width + pair * 2 * head, 2 * head), 2 * head)
            pre = dot(normed_ref[...], wu[:, columns])
            pre_ref[:, columns] = pre
            act = (pre * sigmoid(pre)).astype(BF)
            for b in range(2):
                qkv_send[2 * pair + b, :, slot * head : (slot + 1) * head] = act[
                    :, b * head : (b + 1) * head
                ]
        for b in range(2):
            peer = 2 * pair + b

            @pl.when(peer != c)
            def _(peer=peer):
                chain_copy(qkv_send.at[peer], qkv.at[mine], qkv_ss, qkv_rs, peer).start()

    qkv[mine, :] = qkv_send[c]

    pre = dot(normed_ref[...], wu[:, :width])
    sig = sigmoid(pre)
    gating_ref[...] = (pre * sig).astype(BF)
    pre_ref[:, :width] = sig * (1.0 + pre * (1.0 - sig))
    load_wo.wait()
    gated_grad_ref[...] = dot_nt(ct_ref[...], wo[...])

    def to_slope(step, carry):
        columns = pl.ds(pl.multiple_of(width + step * 512, 512), 512)
        v = pre_ref[:, columns]
        s = sigmoid(v)
        pre_ref[:, columns] = s * (1.0 + v * (1.0 - s))
        return carry

    lax.fori_loop(0, 3 * width // 512, to_slope, 0)

    def await_chain(src, dst, send_sem, recv_sem):
        for away in range(1, n_chain):
            pltpu.make_async_remote_copy(
                src_ref=src,
                dst_ref=dst,
                send_sem=send_sem.at[away],
                recv_sem=recv_sem.at[away],
                device_id=(e, c),
                device_id_type=MESH,
            ).wait_recv()

    def await_sent(src, dst, send_sem, recv_sem):
        for away in range(1, n_chain):
            pltpu.make_async_remote_copy(
                src_ref=src,
                dst_ref=dst,
                send_sem=send_sem.at[away],
                recv_sem=recv_sem.at[away],
                device_id=(e, c),
                device_id_type=MESH,
            ).wait_send()

    await_chain(qkv_send.at[0], qkv.at[pl.ds(0, rows)], qkv_ss, qkv_rs)

    tile = 2 * rows
    tiles = tokens // tile
    lower = iota((tile, tile), 0) >= iota((tile, tile), 1)
    for i in range(tiles):
        at_i = slice(tile * i, tile * (i + 1))
        ids = hist_col[at_i, :]
        ids = jnp.concatenate([ids, ids], axis=1)
        mixed = None
        for j in range(i + 1):
            at_j = slice(tile * j, tile * (j + 1))
            scores = dot_nt(qkv[at_i, :head], qkv[at_j, head : 2 * head]) * alpha
            visible = ids == hist_ref[:, at_j].astype(F32)
            if i == j:
                visible = visible & lower
            sig = sigmoid(scores)
            weights = jnp.where(visible, scores * sig, 0.0).astype(BF)
            att[at_i, at_j] = weights
            slope[at_i, at_j] = jnp.where(
                visible, (alpha * sig) * (1.0 + scores * (1.0 - sig)), 0.0
            )
            term = dot(weights, qkv[at_j, 2 * head :])
            mixed = term if mixed is None else mixed + term
        mix_send[at_i, :] = mixed.astype(BF)
        for b in range(2):
            peer = 2 * i + b

            @pl.when(peer != c)
            def _(peer=peer):
                chain_copy(
                    mix_send.at[pl.ds(peer * rows, rows)], mix_recv.at[c], mix_ss, mix_rs, peer
                ).start()

    mix_recv[c] = mix_send[mine, :]
    await_chain(mix_send.at[pl.ds(0, rows)], mix_recv.at[0], mix_ss, mix_rs)

    mixed = jnp.concatenate([mix_recv[h] for h in range(HEADS)], axis=1).astype(F32)
    center = mixed - mean(mixed)
    inverse = lax.rsqrt(mean(center * center) + epsilon)
    mixed_norm = center * inverse
    gating = gating_ref[...].astype(F32)
    gated_grad = gated_grad_ref[...]
    upstream = gated_grad * gating
    mixed_grad = inverse * (
        upstream - mean(upstream) - mixed_norm * mean(upstream * mixed_norm)
    )
    mixed_grad = mixed_grad.astype(BF)
    for h in range(HEADS):
        mg_send[h] = mixed_grad[:, h * head : (h + 1) * head]
    for away in (4, 3, 5, 2, 6, 1, 7):
        peer = lax.rem(c + away, n_chain)
        chain_copy(mg_send.at[peer], mg.at[mine], mg_ss, mg_rs, peer).start()
    mg[mine, :] = mg_send[c]
    gated_ref[...] = (mixed_norm * gating).astype(BF)
    pg_ref[:, :width] = (gated_grad * mixed_norm * pre_ref[:, :width]).astype(BF)

    grad_scale = 1.0 / math.sqrt(rows * n_dp * n_chain)

    def weight_term(step, carry):
        columns = pl.ds(pl.multiple_of(step * rows, rows), rows)
        wg_send[columns, :] = (
            dot_tn(gated_ref[:, columns], ct_ref[...]) * grad_scale
        ).astype(BF)
        return carry

    lax.fori_loop(0, width // rows, weight_term, 0)
    own_wg = pl.ds(pl.multiple_of(e * share, share), share)
    wg_recv[own_wg, :] = wg_send[own_wg, :]
    lax.fori_loop(1, n_dp, to_group(wg_send, wg_recv, wg_sems, share), 0)

    layer_out_ref[...] = (residual_ref[...] + dot(gated_ref[...], wo[...])).astype(BF)
    ng_ref[...] = dot_nt(pg_ref[:, :width], wu[:, :width])

    await_chain(mg_send.at[0], mg.at[pl.ds(0, rows)], mg_ss, mg_rs)

    for i in range(tiles - 1, -1, -1):
        at_i = slice(tile * i, tile * (i + 1))
        after = slice(tile * i, tokens)
        query_grad = None
        for j in range(i + 1):
            at_j = slice(tile * j, tile * (j + 1))
            grad = dot_nt(mg[at_i, :], qkv[at_j, 2 * head :])
            grad = (grad * slope[at_i, at_j]).astype(BF)
            sgrad[at_i, at_j] = grad
            term = dot(grad, qkv[at_j, head : 2 * head])
            query_grad = term if query_grad is None else query_grad + term
        key_grad = dot_tn(sgrad[after, at_i], qkv[after, :head])
        value_grad = dot_tn(att[after, at_i], mg[after, :])
        grads = jnp.concatenate([query_grad, key_grad, value_grad], axis=1).astype(BF)
        for b in range(2):
            peer = 2 * i + b
            d_send[peer] = grads[rows * b : rows * (b + 1), :]

            @pl.when(peer != c)
            def _(peer=peer):
                chain_copy(d_send.at[peer], d_recv.at[c], d_ss, d_rs, peer).start()

    d_recv[c] = d_send[c]

    await_group(wg_recv, wg_sems.at[1], share)

    def add_up(step, carry):
        here = pl.ds(pl.multiple_of(step * share, share), share)
        return carry + wg_recv[here, :].astype(F32)

    summed = lax.fori_loop(0, n_dp, add_up, jnp.zeros((share, width), F32)).astype(BF)
    for h in range(n_chain):
        part_send[h] = summed[:, h * head : (h + 1) * head]
    for away in (4, 3, 5, 2, 6, 1, 7):
        peer = lax.rem(c + away, n_chain)
        chain_copy(part_send.at[peer], part_recv.at[c], part_ss, part_rs, peer).start()
    part_recv[c] = part_send[c]

    await_chain(d_send.at[0], d_recv.at[0], d_ss, d_rs)
    for slot, part in ((0, 2), (1, 3), (2, 1)):
        for h in range(HEADS):
            columns = slice(part * width + h * head, part * width + (h + 1) * head)
            pg_ref[:, columns] = (
                d_recv[h, :, slot * head : (slot + 1) * head].astype(F32)
                * pre_ref[:, columns]
            ).astype(BF)
    normed_grad = ng_ref[...] + dot_nt(pg_ref[:, width:], wu[:, width:])

    await_chain(part_send.at[0], part_recv.at[0], part_ss, part_rs)
    whole = part_recv[0].astype(F32)
    for h in range(1, n_chain):
        whole = whole + part_recv[h].astype(F32)
    full_send[...] = whole.astype(BF)
    for away in (4, 3, 5, 2, 6, 1, 7):
        peer = lax.rem(c + away, n_chain)
        chain_copy(full_send, full_recv.at[c], full_ss, full_rs, peer).start()
    full_recv[c] = full_send[...]

    residual = residual_ref[...]
    center = residual - mean(residual)
    inverse = lax.rsqrt(mean(center * center) + epsilon)
    normed = center * inverse
    input_grad = ct_ref[...].astype(F32) + inverse * (
        normed_grad - mean(normed_grad) - normed * mean(normed_grad * normed)
    )
    input_grad = input_grad.astype(BF)

    slot_col = ev_recv[:, cols : cols + rows].astype(F32).astype(I32)
    slot_there = slot_col == iota((total, rows), 1)
    quarter = lax.rem(iota((total, rows), 0), block) // per_peer
    back = jnp.concatenate(
        [one_hot(slot_there & (quarter == q)) for q in range(fold)], axis=1
    )
    stacked = jnp.concatenate(
        [input_grad[:, cols * q : cols * (q + 1)] for q in range(fold)], axis=0
    )
    ret_send[...] = dot(back, stacked).astype(BF)
    ret_recv[own_ev, :] = ret_send[own_ev, :]
    lax.fori_loop(1, n_dp, to_group(ret_send, ret_recv, ret_sems, block), 0)

    await_chain(full_send, full_recv.at[0], full_ss, full_rs)
    for h in range(n_chain):
        weight_grad_ref[:, h * head : (h + 1) * head] = full_recv[h].astype(F32)

    await_group(ret_recv, ret_sems.at[1], block)
    returned = ret_recv[...]
    place = jnp.concatenate([place_col] * fold, axis=1)
    here = iota((rows, total), 1)
    for q in range(fold):
        event_grad_ref[:, cols * q : cols * (q + 1)] = dot(
            one_hot(here == place + per_peer * q), returned
        ).astype(BF)

    await_group(ev_send, ev_sems.at[0], block)
    await_group(wg_send, wg_sems.at[0], share)
    await_group(ret_send, ret_sems.at[0], block)
    await_sent(qkv_send.at[0], qkv.at[pl.ds(0, rows)], qkv_ss, qkv_rs)
    await_sent(mix_send.at[pl.ds(0, rows)], mix_recv.at[0], mix_ss, mix_rs)
    await_sent(mg_send.at[0], mg.at[pl.ds(0, rows)], mg_ss, mg_rs)
    await_sent(d_send.at[0], d_recv.at[0], d_ss, d_rs)
    await_sent(part_send.at[0], part_recv.at[0], part_ss, part_rs)
    await_sent(full_send, full_recv.at[0], full_ss, full_rs)


def on_device(n_dp, n_chain, events, destinations, history_ids, cotangent, w_uvqk, w_out):
    _, rows, width = events.shape
    head = width // HEADS
    tokens = rows * n_chain
    per_peer = rows // n_dp
    fold = max(1, 16 // per_peer)
    total = rows * fold
    cols = width // fold
    share = width // n_dp
    vmem = pl.BlockSpec(memory_space=pltpu.VMEM)
    anywhere = pl.BlockSpec(memory_space=pl.ANY)
    pair = pltpu.SemaphoreType.DMA((2,))
    ring = pltpu.SemaphoreType.DMA((n_chain,))
    layer_out, event_grad, weight_grad = pl.pallas_call(
        functools.partial(kernel, n_dp, n_chain),
        out_shape=(
            jax.ShapeDtypeStruct((rows, width), BF),
            jax.ShapeDtypeStruct((rows, width), BF),
            jax.ShapeDtypeStruct((share, width), F32),
        ),
        in_specs=[vmem, vmem, vmem, vmem, anywhere, anywhere],
        out_specs=(vmem, vmem, vmem),
        scratch_shapes=[
            pltpu.VMEM((width, 4 * width), BF),
            pltpu.VMEM((width, width), BF),
            pltpu.VMEM((total, cols + rows), BF),
            pltpu.VMEM((total, cols + rows), BF),
            pltpu.VMEM((rows, width), F32),
            pltpu.VMEM((rows, width), BF),
            pltpu.VMEM((rows, 4 * width), F32),
            pltpu.VMEM((rows, width), BF),
            pltpu.VMEM((rows, width), F32),
            pltpu.VMEM((n_chain, rows, 3 * head), BF),
            pltpu.VMEM((tokens, 3 * head), BF),
            pltpu.VMEM((tokens, rows), F32),
            pltpu.VMEM((tokens, tokens), BF),
            pltpu.VMEM((tokens, tokens), F32),
            pltpu.VMEM((tokens, tokens), BF),
            pltpu.VMEM((tokens, head), BF),
            pltpu.VMEM((n_chain, rows, head), BF),
            pltpu.VMEM((n_chain, rows, head), BF),
            pltpu.VMEM((tokens, head), BF),
            pltpu.VMEM((rows, width), BF),
            pltpu.VMEM((width, width), BF),
            pltpu.VMEM((width, width), BF),
            pltpu.VMEM((n_chain, rows, 3 * head), BF),
            pltpu.VMEM((n_chain, rows, 3 * head), BF),
            pltpu.VMEM((rows, 4 * width), BF),
            pltpu.VMEM((rows, width), F32),
            pltpu.VMEM((n_chain, share, head), BF),
            pltpu.VMEM((n_chain, share, head), BF),
            pltpu.VMEM((share, head), BF),
            pltpu.VMEM((n_chain, share, head), BF),
            pltpu.VMEM((total, cols), BF),
            pltpu.VMEM((total, cols), BF),
            pair,
            pair,
            pair,
            pair,
            pair,
        ]
        + [ring] * 12,
        compiler_params=pltpu.CompilerParams(
            collective_id=0, has_side_effects=True, vmem_limit_bytes=56 * 1024 * 1024
        ),
        cost_estimate=pl.CostEstimate(
            flops=9 * 2**30, bytes_accessed=12 * 2**20, transcendentals=4 * 2**20
        ),
        name="hstu_layer",
    )(events[0], destinations, history_ids, cotangent[0], w_uvqk, w_out)
    return (layer_out[None], event_grad[None], weight_grad)


def solution(mesh):
    return jax.shard_map(
        functools.partial(on_device, mesh.shape["dp"], mesh.shape["chain"]),
        mesh=mesh,
        in_specs=(
            P("dp", "chain", None),
            P("dp", "chain"),
            P("dp", None),
            P("dp", "chain", None),
            P(),
            P(),
        ),
        out_specs=(P("dp", "chain", None), P("dp", "chain", None), P("dp", None)),
        check_vma=False,
    )
```

time: 438 us -> 101 us (0.23)
  waiting for transfers between devices: 265 us -> 0 us
  Pallas kernels: 0 us -> 94.8 us
  starting transfers between devices: 53.6 us -> 0 us
  local copies, waits for them, and re-layouts: 48.3 us -> 4.91 us
  matrix products: 38.8 us -> 0 us
  between operations: 14.2 us -> 0.64 us
  other arithmetic: 12.7 us -> 0 us
    reduce_scatter x2 -> x0, waiting for transfers between devices: 129 us -> none  [the longest x1 69.2 us: on_device(): lax.psum_scatter((lax.dot_general(gated, upstream, (((0,), (0,)), ((), ()...]
    pallas_call x0 -> x1, Pallas kernels: none -> 94.8 us  [on_device(): pl.pallas_call(functools.partial(kernel, n_dp, n_chain), out_shape=(jax.S...]
    psum x1 -> x0, waiting for transfers between devices: 68.7 us -> none  [on_device(): weight_grad = lax.psum(partial_grad, 'chain').astype(jnp.float32)]
    ppermute x7 -> x0, waiting for transfers between devices: 55.3 us -> none  [passed_along(): return lax.ppermute(x, axis, pairs)]
    dot_general x11 -> x0, matrix products: 38.8 us -> none  [the longest x2 9.46 us: contract_last(): lax.dot_general(left_side, right_side, (((1,), (1,)), ((), ())), preferre...]
    ppermute x7 -> x0, starting transfers between devices: 33 us -> none  [passed_along(): return lax.ppermute(x, axis, pairs)]
    all_to_all x3 -> x0, starting transfers between devices: 20.2 us -> none  [the longest x1 8.59 us: on_device(): lax.all_to_all(outgoing_slots.reshape(dp_size, per_peer), 'dp', split_axi...]
    reshape x11 -> x0, local copies, waits for them, and re-layouts: 15.7 us -> none  [the longest x1 3.98 us: on_device(): key_part = jnp.einsum('hqk,qhd->khd', score_grad, queries, preferred_elem...]
  transfers between devices with their start and end apart: 13 -> 0, of which waited for: 12 -> 0; matrix products, arithmetic and copies ran while one was open for 6% -> 0% of each run, Pallas kernels for 0% -> 0%
where the time goes in v1:
time: 101 us; the launch traced here: 100 us
  Pallas kernels  94.8 us (94%)
  local copies, waits for them, and re-layouts  4.91 us (5%)
    pallas_call x1, Pallas kernels, on_device(): pl.pallas_call(functools.partial(kernel, n_dp, n_chain), out_shape=(jax.S...  94.8 us
    unnamed x3, local copies, waits for them, and re-layouts  4.91 us

profile of v1, /device:TPU:1, one launch (start us, length us, event | category | flops | bytes accessed | tf_op | source)
XLA Modules:
  0.0 100.3 jit_solution(13799494291821097176)
XLA Ops:
  0.6 94.8 %hstu_layer.1 = (bf16[128,1024]{1,0:T(8,128)(2,1)}, bf16[128,1024]{1,0:T(8,128)(2,1)}, f32[32,1024]{1,0:T(8,128)}) custom-call(bf16[128,1024]{1,0:T(8,128)(2,1)} %bitcast.6, s32[1,128]{1,0:T(1,128)} %dest_ref.1, s32[1,1024]{1,0:T(1,128)} %hist_ref.1, bf16[128,1024]{1,0:T(8,128)(2,1)} %bitcast.7, bf16[1024,4096]{1,0:T(8,128)(2,1)} %wu_hbm.1, ...), custom_call_target="tpu_custom_call" | custom-call | flops 9663676416 | bytes 12582912 | tf_op jit(solution)/shard_map/hstu_layer/pallas_call | solution.py:495
  95.4 1.7 %copy.12 = bf16[1,128,1024]{2,1,0:T(8,128)(2,1)} copy(bf16[1,128,1024]{2,1,0:T(8,128)(2,1)} %bitcast.5) | data formatting | bytes 524288
  97.1 1.7 %copy.13 = bf16[1,128,1024]{2,1,0:T(8,128)(2,1)} copy(bf16[1,128,1024]{2,1,0:T(8,128)(2,1)} %bitcast.4) | data formatting | bytes 524288
  98.8 1.6 %copy.14 = f32[32,1024]{1,0:T(8,128)} copy(f32[32,1024]{1,0:T(8,128)} %get-tuple-element.14) | data formatting | bytes 262144

commit v2 on v1

--- a/solution.py
+++ b/solution.py
@@ -47,14 +47,18 @@
 def kernel(
     n_dp,
     n_chain,
-    ev_ref,
     dest_ref,
     hist_ref,
-    ct_ref,
+    ev_hbm,
+    ct_hbm,
     wu_hbm,
     wo_hbm,
+    event_grad_ref,
+    layer_out_hbm,
+    weight_grad_hbm,
+    ev_ref,
+    ct_ref,
     layer_out_ref,
-    event_grad_ref,
     weight_grad_ref,
     wu,
     wo,
@@ -77,6 +81,7 @@
     mg,
     gated_ref,
     wg_send,
+    wg_twin,
     wg_recv,
     d_send,
     d_recv,
@@ -89,8 +94,9 @@
     ret_send,
     ret_recv,
     load_sem,
-    local_sem,
+    store_sem,
     ev_sems,
+    twin_sems,
     wg_sems,
     ret_sems,
     qkv_ss,
@@ -119,10 +125,11 @@
     e = lax.axis_index("dp")
     c = lax.axis_index("chain")
 
+    load_ev = pltpu.make_async_copy(ev_hbm, ev_ref, load_sem.at[2])
+    load_ct = pltpu.make_async_copy(ct_hbm, ct_ref, load_sem.at[3])
     load_wu = pltpu.make_async_copy(wu_hbm, wu, load_sem.at[0])
     load_wo = pltpu.make_async_copy(wo_hbm, wo, load_sem.at[1])
-    load_wu.start()
-    load_wo.start()
+    load_ev.start()
 
     barrier = pltpu.get_barrier_semaphore()
 
@@ -137,6 +144,10 @@
         pl.semaphore_signal(
             barrier, inc=1, device_id=(e, lax.rem(c + step, n_chain)), device_id_type=MESH
         )
+
+    load_wu.start()
+    load_ct.start()
+    load_wo.start()
 
     ri = iota((rows, rows), 0)
     ci = iota((rows, rows), 1)
@@ -157,6 +168,7 @@
     spread = jnp.concatenate(
         [one_hot(at == at_row + per_peer * q) for q in range(fold)], axis=1
     )
+    load_ev.wait()
     packed = jnp.concatenate(
         [
             jnp.concatenate([ev_ref[:, cols * q : cols * (q + 1)], slots], axis=1)
@@ -188,8 +200,8 @@
 
         return one
 
-    def await_group(buffer, sem, rows_each):
-        part = buffer.at[pl.ds(0, (n_dp - 1) * rows_each)]
+    def await_group(buffer, sem, rows_each, peers=n_dp - 1):
+        part = buffer.at[pl.ds(0, peers * rows_each)]
         pltpu.make_async_copy(part, part, sem).wait()
 
     lax.fori_loop(1, n_dp, to_group(ev_send, ev_recv, ev_sems, block), 0)
@@ -266,6 +278,7 @@
     gating_ref[...] = (pre * sig).astype(BF)
     pre_ref[:, :width] = sig * (1.0 + pre * (1.0 - sig))
     load_wo.wait()
+    load_ct.wait()
     gated_grad_ref[...] = dot_nt(ct_ref[...], wo[...])
 
     def to_slope(step, carry):
@@ -359,19 +372,58 @@
     grad_scale = 1.0 / math.sqrt(rows * n_dp * n_chain)
 
     def weight_term(step, carry):
-        columns = pl.ds(pl.multiple_of(step * rows, rows), rows)
-        wg_send[columns, :] = (
-            dot_tn(gated_ref[:, columns], ct_ref[...]) * grad_scale
+        columns = pl.ds(pl.multiple_of(step * 4 * share, 4 * share), 4 * share)
+        term = (dot_tn(gated_ref[:, columns], ct_ref[...]) * grad_scale).astype(BF)
+        for b in range(4):
+            to = pl.ds(pl.multiple_of((2 * step + b // 2) * share, share), share)
+            wg_send[b % 2, to, :] = term[b * share : (b + 1) * share, :]
+        return carry
+
+    lax.fori_loop(0, n_dp // 4, weight_term, 0)
+    core = lax.rem(e, 2)
+    twin_copy = pltpu.make_async_remote_copy(
+        src_ref=wg_send.at[1 - core],
+        dst_ref=wg_twin,
+        send_sem=twin_sems.at[0],
+        recv_sem=twin_sems.at[1],
+        device_id=(e + 1 - 2 * core, c),
+        device_id_type=MESH,
+    )
+    twin_copy.start()
+
+    layer_out_ref[...] = (residual_ref[...] + dot(gated_ref[...], wo[...])).astype(BF)
+    store_lo = pltpu.make_async_copy(layer_out_ref, layer_out_hbm, store_sem.at[0])
+    store_lo.start()
+    ng_ref[...] = dot_nt(pg_ref[:, :width], wu[:, :width])
+
+    twin_copy.wait_recv()
+    place_wg = e // 2
+
+    def add_twin(step, carry):
+        here = pl.ds(pl.multiple_of(step * share, share), share)
+        wg_twin[here, :] = (
+            wg_twin[here, :].astype(F32) + wg_send[core, here, :].astype(F32)
         ).astype(BF)
         return carry
 
-    lax.fori_loop(0, width // rows, weight_term, 0)
-    own_wg = pl.ds(pl.multiple_of(e * share, share), share)
-    wg_recv[own_wg, :] = wg_send[own_wg, :]
-    lax.fori_loop(1, n_dp, to_group(wg_send, wg_recv, wg_sems, share), 0)
-
-    layer_out_ref[...] = (residual_ref[...] + dot(gated_ref[...], wo[...])).astype(BF)
-    ng_ref[...] = dot_nt(pg_ref[:, :width], wu[:, :width])
+    lax.fori_loop(0, n_dp // 2, add_twin, 0)
+    own_wg = pl.ds(pl.multiple_of(place_wg * share, share), share)
+    wg_recv[own_wg, :] = wg_twin[own_wg, :]
+
+    def scatter(step, carry):
+        peer = lax.rem(e + 2 * step, n_dp)
+        there = pl.ds(pl.multiple_of(peer // 2 * share, share), share)
+        pltpu.make_async_remote_copy(
+            src_ref=wg_twin.at[there],
+            dst_ref=wg_recv.at[own_wg],
+            send_sem=wg_sems.at[0],
+            recv_sem=wg_sems.at[1],
+            device_id=(peer, c),
+            device_id_type=MESH,
+        ).start()
+        return carry
+
+    lax.fori_loop(1, n_dp // 2, scatter, 0)
 
     await_chain(mg_send.at[0], mg.at[pl.ds(0, rows)], mg_ss, mg_rs)
 
@@ -399,13 +451,13 @@
 
     d_recv[c] = d_send[c]
 
-    await_group(wg_recv, wg_sems.at[1], share)
+    await_group(wg_recv, wg_sems.at[1], share, n_dp // 2 - 1)
 
     def add_up(step, carry):
         here = pl.ds(pl.multiple_of(step * share, share), share)
         return carry + wg_recv[here, :].astype(F32)
 
-    summed = lax.fori_loop(0, n_dp, add_up, jnp.zeros((share, width), F32)).astype(BF)
+    summed = lax.fori_loop(0, n_dp // 2, add_up, jnp.zeros((share, width), F32)).astype(BF)
     for h in range(n_chain):
         part_send[h] = summed[:, h * head : (h + 1) * head]
     for away in (4, 3, 5, 2, 6, 1, 7):
@@ -458,6 +510,8 @@
     await_chain(full_send, full_recv.at[0], full_ss, full_rs)
     for h in range(n_chain):
         weight_grad_ref[:, h * head : (h + 1) * head] = full_recv[h].astype(F32)
+    store_wg = pltpu.make_async_copy(weight_grad_ref, weight_grad_hbm, store_sem.at[1])
+    store_wg.start()
 
     await_group(ret_recv, ret_sems.at[1], block)
     returned = ret_recv[...]
@@ -469,7 +523,8 @@
         ).astype(BF)
 
     await_group(ev_send, ev_sems.at[0], block)
-    await_group(wg_send, wg_sems.at[0], share)
+    await_group(wg_twin, wg_sems.at[0], share, n_dp // 2 - 1)
+    twin_copy.wait_send()
     await_group(ret_send, ret_sems.at[0], block)
     await_sent(qkv_send.at[0], qkv.at[pl.ds(0, rows)], qkv_ss, qkv_rs)
     await_sent(mix_send.at[pl.ds(0, rows)], mix_recv.at[0], mix_ss, mix_rs)
@@ -477,6 +532,14 @@
     await_sent(d_send.at[0], d_recv.at[0], d_ss, d_rs)
     await_sent(part_send.at[0], part_recv.at[0], part_ss, part_rs)
     await_sent(full_send, full_recv.at[0], full_ss, full_rs)
+    store_lo.wait()
+    store_wg.wait()
+
+
+def hand_over(a, b, c, a_out, b_out, c_out):
+    a_out[...] = a[...]
+    b_out[...] = b[...]
+    c_out[...] = c[...]
 
 
 def on_device(n_dp, n_chain, events, destinations, history_ids, cotangent, w_uvqk, w_out):
@@ -492,16 +555,20 @@
     anywhere = pl.BlockSpec(memory_space=pl.ANY)
     pair = pltpu.SemaphoreType.DMA((2,))
     ring = pltpu.SemaphoreType.DMA((n_chain,))
-    layer_out, event_grad, weight_grad = pl.pallas_call(
+    results = pl.pallas_call(
         functools.partial(kernel, n_dp, n_chain),
         out_shape=(
             jax.ShapeDtypeStruct((rows, width), BF),
             jax.ShapeDtypeStruct((rows, width), BF),
             jax.ShapeDtypeStruct((share, width), F32),
         ),
-        in_specs=[vmem, vmem, vmem, vmem, anywhere, anywhere],
-        out_specs=(vmem, vmem, vmem),
+        in_specs=[vmem, vmem, anywhere, anywhere, anywhere, anywhere],
+        out_specs=(vmem, anywhere, anywhere),
         scratch_shapes=[
+            pltpu.VMEM((rows, width), BF),
+            pltpu.VMEM((rows, width), BF),
+            pltpu.VMEM((rows, width), BF),
+            pltpu.VMEM((share, width), F32),
             pltpu.VMEM((width, 4 * width), BF),
             pltpu.VMEM((width, width), BF),
             pltpu.VMEM((total, cols + rows), BF),
@@ -522,8 +589,9 @@
             pltpu.VMEM((n_chain, rows, head), BF),
             pltpu.VMEM((tokens, head), BF),
             pltpu.VMEM((rows, width), BF),
-            pltpu.VMEM((width, width), BF),
-            pltpu.VMEM((width, width), BF),
+            pltpu.VMEM((2, width // 2, width), BF),
+            pltpu.VMEM((width // 2, width), BF),
+            pltpu.VMEM((width // 2, width), BF),
             pltpu.VMEM((n_chain, rows, 3 * head), BF),
             pltpu.VMEM((n_chain, rows, 3 * head), BF),
             pltpu.VMEM((rows, 4 * width), BF),
@@ -534,6 +602,7 @@
             pltpu.VMEM((n_chain, share, head), BF),
             pltpu.VMEM((total, cols), BF),
             pltpu.VMEM((total, cols), BF),
+            pltpu.SemaphoreType.DMA((4,)),
             pair,
             pair,
             pair,
@@ -548,7 +617,14 @@
             flops=9 * 2**30, bytes_accessed=12 * 2**20, transcendentals=4 * 2**20
         ),
         name="hstu_layer",
-    )(events[0], destinations, history_ids, cotangent[0], w_uvqk, w_out)
+    )(destinations, history_ids, events[0], cotangent[0], w_uvqk, w_out)
+    event_grad, layer_out, weight_grad = pl.pallas_call(
+        hand_over,
+        out_shape=tuple(jax.ShapeDtypeStruct(r.shape, r.dtype) for r in results),
+        in_specs=[vmem] * 3,
+        out_specs=(vmem,) * 3,
+        name="hand_over",
+    )(*results)
     return (layer_out[None], event_grad[None], weight_grad)
 
 

time: 101 us -> 90.6 us (0.90)
  Pallas kernels: 94.8 us -> 89.8 us
  local copies, waits for them, and re-layouts: 4.91 us -> 0 us
    pallas_call x1, Pallas kernels: 94.8 us -> 87.9 us  [on_device(): pl.pallas_call(functools.partial(kernel, n_dp, n_chain), out_shape=(jax.S...]
    unnamed x3 -> x0, local copies, waits for them, and re-layouts: 4.91 us -> none
    pallas_call x0 -> x1, Pallas kernels: none -> 1.91 us  [on_device(): pl.pallas_call(hand_over, out_shape=tuple((jax.ShapeDtypeStruct(r.shape,...]
where the time goes in v2:
time: 90.6 us; the launch traced here: 90.5 us
  Pallas kernels  89.8 us (99%)
    pallas_call x1, Pallas kernels, on_device(): pl.pallas_call(functools.partial(kernel, n_dp, n_chain), out_shape=(jax.S...  87.9 us
    pallas_call x1, Pallas kernels, on_device(): pl.pallas_call(hand_over, out_shape=tuple((jax.ShapeDtypeStruct(r.shape,...  1.91 us

profile of v2, /device:TPU:1, one launch (start us, length us, event | category | flops | bytes accessed | tf_op | source)
XLA Modules:
  0.0 90.5 jit_solution(5508633427997338033)
XLA Ops:
  0.6 87.9 %hstu_layer.1 = (bf16[128,1024]{1,0:T(8,128)(2,1)}, bf16[128,1024]{1,0:T(8,128)(2,1)}, f32[32,1024]{1,0:T(8,128)}) custom-call(s32[1,128]{1,0:T(1,128)} %dest_ref.1, s32[1,1024]{1,0:T(1,128)} %hist_ref.1, bf16[128,1024]{1,0:T(8,128)(2,1)} %bitcast.4, bf16[128,1024]{1,0:T(8,128)(2,1)} %bitcast.5, bf16[1024,4096]{1,0:T(8,128)(2,1)} %wu_hbm.1, ...), custom_call_target="tpu_custom_call" | custom-call | flops 9663676416 | bytes 12582912 | tf_op jit(solution)/shard_map/hstu_layer/pallas_call | solution.py:558
  88.6 1.9 %hand_over.1 = (bf16[128,1024]{1,0:T(8,128)(2,1)}, bf16[128,1024]{1,0:T(8,128)(2,1)}, f32[32,1024]{1,0:T(8,128)}) custom-call(bf16[128,1024]{1,0:T(8,128)(2,1)} %get-tuple-element.9.a, bf16[128,1024]{1,0:T(8,128)(2,1)} %get-tuple-element.10.b, f32[32,1024]{1,0:T(8,128)} %get-tuple-element.11.c), custom_call_target="tpu_custom_call" | custom-call | tf_op jit(solution)/shard_map/hand_over/pallas_call | solution.py:621

commit v3 on v2

--- a/solution.py
+++ b/solution.py
@@ -57,7 +57,7 @@
     layer_out_hbm,
     weight_grad_hbm,
     ev_ref,
-    ct_ref,
+    ct_all,
     layer_out_ref,
     weight_grad_ref,
     wu,
@@ -77,11 +77,19 @@
     sgrad,
     mix_send,
     mix_recv,
-    mg_send,
+    h_send,
+    h_recv,
+    stat_send,
+    stat_recv,
+    mix_t,
+    key_t,
+    value_t,
+    mg_t,
     mg,
     gated_ref,
+    gt_send,
+    gt_recv,
     wg_send,
-    wg_twin,
     wg_recv,
     d_send,
     d_recv,
@@ -91,20 +99,27 @@
     part_recv,
     full_send,
     full_recv,
+    back_ref,
+    home_ref,
+    inverse_ref,
     ret_send,
     ret_recv,
     load_sem,
     store_sem,
     ev_sems,
-    twin_sems,
-    wg_sems,
+    ct_sems,
+    gt_sems,
+    wg_ss,
+    wg_rs,
     ret_sems,
     qkv_ss,
     qkv_rs,
     mix_ss,
     mix_rs,
-    mg_ss,
-    mg_rs,
+    h_ss,
+    h_rs,
+    stat_ss,
+    stat_rs,
     d_ss,
     d_rs,
     part_ss,
@@ -124,6 +139,10 @@
     share = width // n_dp
     e = lax.axis_index("dp")
     c = lax.axis_index("chain")
+    team = width // rows
+    teams = n_dp // team
+    seat = lax.rem(e, team)
+    ct_ref = ct_all.at[pl.ds(pl.multiple_of(seat * rows, rows), rows)]
 
     load_ev = pltpu.make_async_copy(ev_hbm, ev_ref, load_sem.at[2])
     load_ct = pltpu.make_async_copy(ct_hbm, ct_ref, load_sem.at[3])
@@ -214,7 +233,20 @@
             jnp.sum(jnp.where(eye, ids, 0.0), axis=1, keepdims=True), (rows, rows)
         )
 
+    def to_team(src, dst, sems):
+        for step in range(1, team):
+            other = lax.rem(seat + step, team)
+            pltpu.make_async_remote_copy(
+                src_ref=src(other),
+                dst_ref=dst,
+                send_sem=sems.at[0],
+                recv_sem=sems.at[1],
+                device_id=(e - seat + other, c),
+                device_id_type=MESH,
+            ).start()
+
     await_group(ev_recv, ev_sems.at[1], block)
+    load_ct.wait()
     slot_col = ev_recv[:, cols : cols + rows].astype(F32).astype(I32)
     slot_row = jnp.concatenate(
         [
@@ -278,8 +310,17 @@
     gating_ref[...] = (pre * sig).astype(BF)
     pre_ref[:, :width] = sig * (1.0 + pre * (1.0 - sig))
     load_wo.wait()
-    load_ct.wait()
-    gated_grad_ref[...] = dot_nt(ct_ref[...], wo[...])
+    gated_grad = dot_nt(ct_ref[...], wo[...])
+    gated_grad_ref[...] = gated_grad
+    upstream = gated_grad * gating_ref[...].astype(F32)
+    upstream = (upstream - mean(upstream)).astype(BF)
+    for h in range(HEADS):
+        h_send[h] = upstream[:, h * head : (h + 1) * head]
+    for away in (4, 3, 5, 2, 6, 1, 7):
+        peer = lax.rem(c + away, n_chain)
+        chain_copy(h_send.at[peer], h_recv.at[mine], h_ss, h_rs, peer).start()
+    h_recv[mine, :] = h_send[c]
+    to_team(lambda other: ct_ref, ct_ref, ct_sems)
 
     def to_slope(step, carry):
         columns = pl.ds(pl.multiple_of(width + step * 512, 512), 512)
@@ -290,16 +331,19 @@
 
     lax.fori_loop(0, 3 * width // 512, to_slope, 0)
 
+    def await_one(src, dst, send_sem, recv_sem, away):
+        pltpu.make_async_remote_copy(
+            src_ref=src,
+            dst_ref=dst,
+            send_sem=send_sem.at[away],
+            recv_sem=recv_sem.at[away],
+            device_id=(e, c),
+            device_id_type=MESH,
+        ).wait_recv()
+
     def await_chain(src, dst, send_sem, recv_sem):
         for away in range(1, n_chain):
-            pltpu.make_async_remote_copy(
-                src_ref=src,
-                dst_ref=dst,
-                send_sem=send_sem.at[away],
-                recv_sem=recv_sem.at[away],
-                device_id=(e, c),
-                device_id_type=MESH,
-            ).wait_recv()
+            await_one(src, dst, send_sem, recv_sem, away)
 
     def await_sent(src, dst, send_sem, recv_sem):
         for away in range(1, n_chain):
@@ -316,148 +360,164 @@
 
     tile = 2 * rows
     tiles = tokens // tile
-    lower = iota((tile, tile), 0) >= iota((tile, tile), 1)
+    key_t[...] = qkv[:, head : 2 * head].T
+    value_t[...] = qkv[:, 2 * head :].T
+    upper = iota((tile, tile), 0) <= iota((tile, tile), 1)
     for i in range(tiles):
         at_i = slice(tile * i, tile * (i + 1))
-        ids = hist_col[at_i, :]
-        ids = jnp.concatenate([ids, ids], axis=1)
-        mixed = None
+        until = slice(0, tile * (i + 1))
+        query_ids = hist_ref[:, at_i].astype(F32)
         for j in range(i + 1):
             at_j = slice(tile * j, tile * (j + 1))
-            scores = dot_nt(qkv[at_i, :head], qkv[at_j, head : 2 * head]) * alpha
-            visible = ids == hist_ref[:, at_j].astype(F32)
+            scores = dot_nt(qkv[at_j, head : 2 * head], qkv[at_i, :head]) * alpha
+            ids = hist_col[at_j, :]
+            visible = jnp.concatenate([ids, ids], axis=1) == query_ids
             if i == j:
-                visible = visible & lower
+                visible = visible & upper
             sig = sigmoid(scores)
-            weights = jnp.where(visible, scores * sig, 0.0).astype(BF)
-            att[at_i, at_j] = weights
-            slope[at_i, at_j] = jnp.where(
+            att[at_j, at_i] = jnp.where(visible, scores * sig, 0.0).astype(BF)
+            slope[at_j, at_i] = jnp.where(
                 visible, (alpha * sig) * (1.0 + scores * (1.0 - sig)), 0.0
             )
-            term = dot(weights, qkv[at_j, 2 * head :])
-            mixed = term if mixed is None else mixed + term
-        mix_send[at_i, :] = mixed.astype(BF)
+        mix_t[:, at_i] = dot(value_t[:, until], att[until, at_i])
+
+    await_chain(h_send.at[0], h_recv.at[pl.ds(0, rows)], h_ss, h_rs)
+    mixed = mix_t[...]
+    upstream = h_recv[...].astype(F32).T
+    own_mean = jnp.mean(mixed, axis=0, keepdims=True)
+    center = mixed - own_mean
+    half = tokens // 2
+    stats = jnp.zeros((8, half), F32)
+    line_no = iota((8, half), 0)
+    for k, stat in enumerate(
+        (
+            own_mean,
+            jnp.sum(center * center, axis=0, keepdims=True),
+            jnp.sum(upstream, axis=0, keepdims=True),
+            jnp.sum(upstream * center, axis=0, keepdims=True),
+        )
+    ):
+        stats = jnp.where(line_no == k, stat[:, :half], stats)
+        stats = jnp.where(line_no == 4 + k, stat[:, half:], stats)
+    stat_send[...] = stats
+    for away in (4, 3, 5, 2, 6, 1, 7):
+        peer = lax.rem(c + away, n_chain)
+        chain_copy(stat_send, stat_recv.at[c], stat_ss, stat_rs, peer).start()
+    stat_recv[c] = stats
+
+    for i in range(tiles):
+        at_i = slice(tile * i, tile * (i + 1))
+        mix_send[at_i, :] = mix_t[:, at_i].T.astype(BF)
+    for away in (4, 3, 5, 2, 6, 1, 7):
+        peer = lax.rem(c + away, n_chain)
+        there = pl.ds(pl.multiple_of(peer * rows, rows), rows)
+        chain_copy(mix_send.at[there], mix_recv.at[c], mix_ss, mix_rs, peer).start()
+    mix_recv[c] = mix_send[mine, :]
+
+    await_chain(stat_send, stat_recv.at[0], stat_ss, stat_rs)
+    halves = []
+    for k in range(2):
+        means, squares, sums, products = (
+            [stat_recv[h, 4 * k + n : 4 * k + n + 1, :] for h in range(HEADS)] for n in range(4)
+        )
+        middle = sum(means) / HEADS
+        squares = sum(squares) + head * sum((m - middle) * (m - middle) for m in means)
+        products = sum(products) + sum(u * (m - middle) for u, m in zip(sums, means))
+        inverse = lax.rsqrt(squares / width + epsilon)
+        tilt = inverse * inverse * inverse * (products / width)
+        halves.append((middle, inverse, sum(sums) / width, tilt))
+    middle, inverse, lift, tilt = (
+        jnp.concatenate([halves[0][n], halves[1][n]], axis=1) for n in range(4)
+    )
+    mixed_grad = inverse * (upstream - lift) - tilt * (mix_t[...] - middle)
+    mg_t[...] = mixed_grad.astype(BF)
+    mg[...] = mixed_grad.T.astype(BF)
+
+    for i in range(tiles - 1, -1, -1):
+        at_i = slice(tile * i, tile * (i + 1))
+        until = slice(0, tile * (i + 1))
+        after = slice(tile * i, tokens)
+        for j in range(i + 1):
+            at_j = slice(tile * j, tile * (j + 1))
+            grad = dot(qkv[at_j, 2 * head :], mg_t[:, at_i])
+            sgrad[at_j, at_i] = (grad * slope[at_j, at_i]).astype(BF)
+        query_grad = dot(key_t[:, until], sgrad[until, at_i]).T
+        key_grad = dot(sgrad[at_i, after], qkv[after, :head])
+        value_grad = dot(att[at_i, after], mg[after, :])
+        grads = jnp.concatenate([query_grad, key_grad, value_grad], axis=1).astype(BF)
         for b in range(2):
             peer = 2 * i + b
-
-            @pl.when(peer != c)
-            def _(peer=peer):
-                chain_copy(
-                    mix_send.at[pl.ds(peer * rows, rows)], mix_recv.at[c], mix_ss, mix_rs, peer
-                ).start()
-
-    mix_recv[c] = mix_send[mine, :]
+            d_send[peer] = grads[rows * b : rows * (b + 1), :]
+
+    def send_grads(*distances):
+        for away in distances:
+            peer = lax.rem(c + away, n_chain)
+            chain_copy(d_send.at[peer], d_recv.at[c], d_ss, d_rs, peer).start()
+
+    send_grads(1, 7, 2, 6)
+    d_recv[c] = d_send[c]
+
     await_chain(mix_send.at[pl.ds(0, rows)], mix_recv.at[0], mix_ss, mix_rs)
-
     mixed = jnp.concatenate([mix_recv[h] for h in range(HEADS)], axis=1).astype(F32)
     center = mixed - mean(mixed)
-    inverse = lax.rsqrt(mean(center * center) + epsilon)
-    mixed_norm = center * inverse
+    mixed_norm = center * lax.rsqrt(mean(center * center) + epsilon)
     gating = gating_ref[...].astype(F32)
     gated_grad = gated_grad_ref[...]
-    upstream = gated_grad * gating
-    mixed_grad = inverse * (
-        upstream - mean(upstream) - mixed_norm * mean(upstream * mixed_norm)
-    )
-    mixed_grad = mixed_grad.astype(BF)
-    for h in range(HEADS):
-        mg_send[h] = mixed_grad[:, h * head : (h + 1) * head]
-    for away in (4, 3, 5, 2, 6, 1, 7):
-        peer = lax.rem(c + away, n_chain)
-        chain_copy(mg_send.at[peer], mg.at[mine], mg_ss, mg_rs, peer).start()
-    mg[mine, :] = mg_send[c]
     gated_ref[...] = (mixed_norm * gating).astype(BF)
     pg_ref[:, :width] = (gated_grad * mixed_norm * pre_ref[:, :width]).astype(BF)
 
-    grad_scale = 1.0 / math.sqrt(rows * n_dp * n_chain)
-
-    def weight_term(step, carry):
-        columns = pl.ds(pl.multiple_of(step * 4 * share, 4 * share), 4 * share)
-        term = (dot_tn(gated_ref[:, columns], ct_ref[...]) * grad_scale).astype(BF)
-        for b in range(4):
-            to = pl.ds(pl.multiple_of((2 * step + b // 2) * share, share), share)
-            wg_send[b % 2, to, :] = term[b * share : (b + 1) * share, :]
-        return carry
-
-    lax.fori_loop(0, n_dp // 4, weight_term, 0)
-    core = lax.rem(e, 2)
-    twin_copy = pltpu.make_async_remote_copy(
-        src_ref=wg_send.at[1 - core],
-        dst_ref=wg_twin,
-        send_sem=twin_sems.at[0],
-        recv_sem=twin_sems.at[1],
-        device_id=(e + 1 - 2 * core, c),
-        device_id_type=MESH,
-    )
-    twin_copy.start()
+    for h in range(team):
+        gt_send[h] = gated_ref[:, h * rows : (h + 1) * rows]
+    own_gt = pl.ds(pl.multiple_of(seat * rows, rows), rows)
+    to_team(lambda other: gt_send.at[other], gt_recv.at[own_gt], gt_sems)
+    gt_recv[own_gt, :] = gt_send[seat]
+    send_grads(3, 5)
 
     layer_out_ref[...] = (residual_ref[...] + dot(gated_ref[...], wo[...])).astype(BF)
     store_lo = pltpu.make_async_copy(layer_out_ref, layer_out_hbm, store_sem.at[0])
     store_lo.start()
     ng_ref[...] = dot_nt(pg_ref[:, :width], wu[:, :width])
 
-    twin_copy.wait_recv()
-    place_wg = e // 2
-
-    def add_twin(step, carry):
-        here = pl.ds(pl.multiple_of(step * share, share), share)
-        wg_twin[here, :] = (
-            wg_twin[here, :].astype(F32) + wg_send[core, here, :].astype(F32)
-        ).astype(BF)
-        return carry
-
-    lax.fori_loop(0, n_dp // 2, add_twin, 0)
-    own_wg = pl.ds(pl.multiple_of(place_wg * share, share), share)
-    wg_recv[own_wg, :] = wg_twin[own_wg, :]
-
-    def scatter(step, carry):
-        peer = lax.rem(e + 2 * step, n_dp)
-        there = pl.ds(pl.multiple_of(peer // 2 * share, share), share)
-        pltpu.make_async_remote_copy(
-            src_ref=wg_twin.at[there],
-            dst_ref=wg_recv.at[own_wg],
-            send_sem=wg_sems.at[0],
-            recv_sem=wg_sems.at[1],
-            device_id=(peer, c),
+    await_group(ct_all, ct_sems.at[1], rows, team - 1)
+    await_group(gt_recv, gt_sems.at[1], rows, team - 1)
+    grad_scale = 1.0 / math.sqrt(rows * n_dp * n_chain)
+    term = (dot_tn(gt_recv[...], ct_all[...]) * grad_scale).astype(BF)
+    line = e // team
+
+    def wg_copy(k, owner):
+        return pltpu.make_async_remote_copy(
+            src_ref=wg_send.at[k],
+            dst_ref=wg_recv.at[line],
+            send_sem=wg_ss.at[k],
+            recv_sem=wg_rs.at[line],
+            device_id=(owner, c),
             device_id_type=MESH,
-        ).start()
-        return carry
-
-    lax.fori_loop(1, n_dp // 2, scatter, 0)
-
-    await_chain(mg_send.at[0], mg.at[pl.ds(0, rows)], mg_ss, mg_rs)
-
-    for i in range(tiles - 1, -1, -1):
-        at_i = slice(tile * i, tile * (i + 1))
-        after = slice(tile * i, tokens)
-        query_grad = None
-        for j in range(i + 1):
-            at_j = slice(tile * j, tile * (j + 1))
-            grad = dot_nt(mg[at_i, :], qkv[at_j, 2 * head :])
-            grad = (grad * slope[at_i, at_j]).astype(BF)
-            sgrad[at_i, at_j] = grad
-            term = dot(grad, qkv[at_j, head : 2 * head])
-            query_grad = term if query_grad is None else query_grad + term
-        key_grad = dot_tn(sgrad[after, at_i], qkv[after, :head])
-        value_grad = dot_tn(att[after, at_i], mg[after, :])
-        grads = jnp.concatenate([query_grad, key_grad, value_grad], axis=1).astype(BF)
-        for b in range(2):
-            peer = 2 * i + b
-            d_send[peer] = grads[rows * b : rows * (b + 1), :]
-
-            @pl.when(peer != c)
-            def _(peer=peer):
-                chain_copy(d_send.at[peer], d_recv.at[c], d_ss, d_rs, peer).start()
-
-    d_recv[c] = d_send[c]
-
-    await_group(wg_recv, wg_sems.at[1], share, n_dp // 2 - 1)
-
-    def add_up(step, carry):
-        here = pl.ds(pl.multiple_of(step * share, share), share)
-        return carry + wg_recv[here, :].astype(F32)
-
-    summed = lax.fori_loop(0, n_dp // 2, add_up, jnp.zeros((share, width), F32)).astype(BF)
+        )
+
+    for k in range(teams):
+        wg_send[k] = term[k * share : (k + 1) * share, :]
+        owner = seat * teams + k
+
+        @pl.when(owner != e)
+        def _(k=k, owner=owner):
+            wg_copy(k, owner).start()
+
+        @pl.when(owner == e)
+        def _(k=k):
+            wg_recv[line] = wg_send[k]
+
+    send_grads(4)
+
+    summed = None
+    for k in range(teams):
+        @pl.when(k * team + e // teams != e)
+        def _(k=k):
+            pltpu.make_async_copy(wg_recv.at[k], wg_recv.at[k], wg_rs.at[k]).wait()
+
+    for k in range(teams):
+        part = wg_recv[k].astype(F32)
+        summed = part if summed is None else summed + part
+    summed = summed.astype(BF)
     for h in range(n_chain):
         part_send[h] = summed[:, h * head : (h + 1) * head]
     for away in (4, 3, 5, 2, 6, 1, 7):
@@ -465,15 +525,58 @@
         chain_copy(part_send.at[peer], part_recv.at[c], part_ss, part_rs, peer).start()
     part_recv[c] = part_send[c]
 
-    await_chain(d_send.at[0], d_recv.at[0], d_ss, d_rs)
-    for slot, part in ((0, 2), (1, 3), (2, 1)):
-        for h in range(HEADS):
-            columns = slice(part * width + h * head, part * width + (h + 1) * head)
-            pg_ref[:, columns] = (
-                d_recv[h, :, slot * head : (slot + 1) * head].astype(F32)
-                * pre_ref[:, columns]
-            ).astype(BF)
-    normed_grad = ng_ref[...] + dot_nt(pg_ref[:, width:], wu[:, width:])
+    residual = residual_ref[...]
+    center = residual - mean(residual)
+    inverse = lax.rsqrt(mean(center * center) + epsilon)
+    residual_ref[...] = center * inverse
+    inverse_ref[...] = jnp.broadcast_to(inverse, (rows, rows))
+    slot_col = ev_recv[:, cols : cols + rows].astype(F32).astype(I32)
+    slot_there = slot_col == iota((total, rows), 1)
+    quarter = lax.rem(iota((total, rows), 0), block) // per_peer
+    for q in range(fold):
+        back_ref[:, q * rows : (q + 1) * rows] = one_hot(slot_there & (quarter == q))
+    place = jnp.concatenate([place_col] * fold, axis=1)
+    here = iota((rows, total), 1)
+    for q in range(fold):
+        home_ref[q] = one_hot(here == place + per_peer * q)
+
+    for pair in ((0, 1), (7, 2), (6, 3), (5, 4)):
+        for away in pair:
+            if away:
+                await_one(d_send.at[0], d_recv.at[0], d_ss, d_rs, away)
+        froms = [lax.rem(c - away + n_chain, n_chain) for away in pair]
+        terms = []
+        for slot, part in ((0, 2), (1, 3), (2, 1)):
+            spans = [
+                pl.ds(pl.multiple_of(part * width + h * head, head), head) for h in froms
+            ]
+            grads = [
+                (
+                    d_recv[h, :, slot * head : (slot + 1) * head].astype(F32)
+                    * pre_ref[:, span]
+                ).astype(BF)
+                for h, span in zip(froms, spans)
+            ]
+            terms.append(
+                dot_nt(
+                    jnp.concatenate(grads, axis=1),
+                    jnp.concatenate([wu[:, span] for span in spans], axis=1),
+                )
+            )
+        ng_ref[...] += terms[0] + terms[1] + terms[2]
+    normed_grad = ng_ref[...]
+    normed = residual_ref[...]
+    input_grad = ct_ref[...].astype(F32) + inverse_ref[:, :1] * (
+        normed_grad - mean(normed_grad) - normed * mean(normed_grad * normed)
+    )
+    input_grad = input_grad.astype(BF)
+
+    stacked = jnp.concatenate(
+        [input_grad[:, cols * q : cols * (q + 1)] for q in range(fold)], axis=0
+    )
+    ret_send[...] = dot(back_ref[...], stacked).astype(BF)
+    ret_recv[own_ev, :] = ret_send[own_ev, :]
+    lax.fori_loop(1, n_dp, to_group(ret_send, ret_recv, ret_sems, block), 0)
 
     await_chain(part_send.at[0], part_recv.at[0], part_ss, part_rs)
     whole = part_recv[0].astype(F32)
@@ -485,27 +588,10 @@
         chain_copy(full_send, full_recv.at[c], full_ss, full_rs, peer).start()
     full_recv[c] = full_send[...]
 
-    residual = residual_ref[...]
-    center = residual - mean(residual)
-    inverse = lax.rsqrt(mean(center * center) + epsilon)
-    normed = center * inverse
-    input_grad = ct_ref[...].astype(F32) + inverse * (
-        normed_grad - mean(normed_grad) - normed * mean(normed_grad * normed)
-    )
-    input_grad = input_grad.astype(BF)
-
-    slot_col = ev_recv[:, cols : cols + rows].astype(F32).astype(I32)
-    slot_there = slot_col == iota((total, rows), 1)
-    quarter = lax.rem(iota((total, rows), 0), block) // per_peer
-    back = jnp.concatenate(
-        [one_hot(slot_there & (quarter == q)) for q in range(fold)], axis=1
-    )
-    stacked = jnp.concatenate(
-        [input_grad[:, cols * q : cols * (q + 1)] for q in range(fold)], axis=0
-    )
-    ret_send[...] = dot(back, stacked).astype(BF)
-    ret_recv[own_ev, :] = ret_send[own_ev, :]
-    lax.fori_loop(1, n_dp, to_group(ret_send, ret_recv, ret_sems, block), 0)
+    await_group(ret_recv, ret_sems.at[1], block)
+    returned = ret_recv[...]
+    for q in range(fold):
+        event_grad_ref[:, cols * q : cols * (q + 1)] = dot(home_ref[q], returned).astype(BF)
 
     await_chain(full_send, full_recv.at[0], full_ss, full_rs)
     for h in range(n_chain):
@@ -513,22 +599,19 @@
     store_wg = pltpu.make_async_copy(weight_grad_ref, weight_grad_hbm, store_sem.at[1])
     store_wg.start()
 
-    await_group(ret_recv, ret_sems.at[1], block)
-    returned = ret_recv[...]
-    place = jnp.concatenate([place_col] * fold, axis=1)
-    here = iota((rows, total), 1)
-    for q in range(fold):
-        event_grad_ref[:, cols * q : cols * (q + 1)] = dot(
-            one_hot(here == place + per_peer * q), returned
-        ).astype(BF)
-
     await_group(ev_send, ev_sems.at[0], block)
-    await_group(wg_twin, wg_sems.at[0], share, n_dp // 2 - 1)
-    twin_copy.wait_send()
+    await_group(ct_all, ct_sems.at[0], rows, team - 1)
+    await_group(gt_recv, gt_sems.at[0], rows, team - 1)
+    for k in range(teams):
+        @pl.when(seat * teams + k != e)
+        def _(k=k):
+            pltpu.make_async_copy(wg_send.at[k], wg_send.at[k], wg_ss.at[k]).wait()
+
     await_group(ret_send, ret_sems.at[0], block)
     await_sent(qkv_send.at[0], qkv.at[pl.ds(0, rows)], qkv_ss, qkv_rs)
     await_sent(mix_send.at[pl.ds(0, rows)], mix_recv.at[0], mix_ss, mix_rs)
-    await_sent(mg_send.at[0], mg.at[pl.ds(0, rows)], mg_ss, mg_rs)
+    await_sent(h_send.at[0], h_recv.at[pl.ds(0, rows)], h_ss, h_rs)
+    await_sent(stat_send, stat_recv.at[0], stat_ss, stat_rs)
     await_sent(d_send.at[0], d_recv.at[0], d_ss, d_rs)
     await_sent(part_send.at[0], part_recv.at[0], part_ss, part_rs)
     await_sent(full_send, full_recv.at[0], full_ss, full_rs)
@@ -554,6 +637,7 @@
     vmem = pl.BlockSpec(memory_space=pltpu.VMEM)
     anywhere = pl.BlockSpec(memory_space=pl.ANY)
     pair = pltpu.SemaphoreType.DMA((2,))
+    quad = pltpu.SemaphoreType.DMA((rows // share,))
     ring = pltpu.SemaphoreType.DMA((n_chain,))
     results = pl.pallas_call(
         functools.partial(kernel, n_dp, n_chain),
@@ -566,7 +650,7 @@
         out_specs=(vmem, anywhere, anywhere),
         scratch_shapes=[
             pltpu.VMEM((rows, width), BF),
-            pltpu.VMEM((rows, width), BF),
+            pltpu.VMEM((width, width), BF),
             pltpu.VMEM((rows, width), BF),
             pltpu.VMEM((share, width), F32),
             pltpu.VMEM((width, 4 * width), BF),
@@ -588,10 +672,18 @@
             pltpu.VMEM((n_chain, rows, head), BF),
             pltpu.VMEM((n_chain, rows, head), BF),
             pltpu.VMEM((tokens, head), BF),
+            pltpu.VMEM((8, tokens // 2), F32),
+            pltpu.VMEM((n_chain, 8, tokens // 2), F32),
+            pltpu.VMEM((head, tokens), F32),
+            pltpu.VMEM((head, tokens), BF),
+            pltpu.VMEM((head, tokens), BF),
+            pltpu.VMEM((head, tokens), BF),
+            pltpu.VMEM((tokens, head), BF),
             pltpu.VMEM((rows, width), BF),
-            pltpu.VMEM((2, width // 2, width), BF),
-            pltpu.VMEM((width // 2, width), BF),
-            pltpu.VMEM((width // 2, width), BF),
+            pltpu.VMEM((width // rows, rows, rows), BF),
+            pltpu.VMEM((width, rows), BF),
+            pltpu.VMEM((rows // share, share, width), BF),
+            pltpu.VMEM((rows // share, share, width), BF),
             pltpu.VMEM((n_chain, rows, 3 * head), BF),
             pltpu.VMEM((n_chain, rows, 3 * head), BF),
             pltpu.VMEM((rows, 4 * width), BF),
@@ -600,6 +692,9 @@
             pltpu.VMEM((n_chain, share, head), BF),
             pltpu.VMEM((share, head), BF),
             pltpu.VMEM((n_chain, share, head), BF),
+            pltpu.VMEM((total, total), BF),
+            pltpu.VMEM((fold, rows, total), BF),
+            pltpu.VMEM((rows, rows), F32),
             pltpu.VMEM((total, cols), BF),
             pltpu.VMEM((total, cols), BF),
             pltpu.SemaphoreType.DMA((4,)),
@@ -607,9 +702,11 @@
             pair,
             pair,
             pair,
+            quad,
+            quad,
             pair,
         ]
-        + [ring] * 12,
+        + [ring] * 14,
         compiler_params=pltpu.CompilerParams(
             collective_id=0, has_side_effects=True, vmem_limit_bytes=56 * 1024 * 1024
         ),

time: 90.6 us -> 85.6 us (0.945)
  Pallas kernels: 89.8 us -> 84.8 us
    pallas_call x1, Pallas kernels: 87.9 us -> 82.9 us  [on_device(): pl.pallas_call(functools.partial(kernel, n_dp, n_chain), out_shape=(jax.S...]
where the time goes in v3:
time: 85.6 us; the launch traced here: 85.5 us
  Pallas kernels  84.8 us (99%)
    pallas_call x1, Pallas kernels, on_device(): pl.pallas_call(functools.partial(kernel, n_dp, n_chain), out_shape=(jax.S...  82.9 us
    pallas_call x1, Pallas kernels, on_device(): pl.pallas_call(hand_over, out_shape=tuple((jax.ShapeDtypeStruct(r.shape,...  1.91 us

profile of v3, /device:TPU:1, one launch (start us, length us, event | category | flops | bytes accessed | tf_op | source)
XLA Modules:
  0.0 85.5 jit_solution(7333323816719877262)
XLA Ops:
  0.6 82.9 %hstu_layer.1 = (bf16[128,1024]{1,0:T(8,128)(2,1)}, bf16[128,1024]{1,0:T(8,128)(2,1)}, f32[32,1024]{1,0:T(8,128)}) custom-call(s32[1,128]{1,0:T(1,128)} %dest_ref.1, s32[1,1024]{1,0:T(1,128)} %hist_ref.1, bf16[128,1024]{1,0:T(8,128)(2,1)} %bitcast.4, bf16[128,1024]{1,0:T(8,128)(2,1)} %bitcast.5, bf16[1024,4096]{1,0:T(8,128)(2,1)} %wu_hbm.1, ...), custom_call_target="tpu_custom_call" | custom-call | flops 9663676416 | bytes 12582912 | tf_op jit(solution)/shard_map/hstu_layer/pallas_call | solution.py:642
  83.5 1.9 %hand_over.1 = (bf16[128,1024]{1,0:T(8,128)(2,1)}, bf16[128,1024]{1,0:T(8,128)(2,1)}, f32[32,1024]{1,0:T(8,128)}) custom-call(bf16[128,1024]{1,0:T(8,128)(2,1)} %get-tuple-element.9.a, bf16[128,1024]{1,0:T(8,128)(2,1)} %get-tuple-element.10.b, f32[32,1024]{1,0:T(8,128)} %get-tuple-element.11.c), custom_call_target="tpu_custom_call" | custom-call | tf_op jit(solution)/shard_map/hand_over/pallas_call | solution.py:718

commit v4 on v3

--- a/solution.py
+++ b/solution.py
@@ -47,17 +47,20 @@
 def kernel(
     n_dp,
     n_chain,
-    dest_ref,
-    hist_ref,
+    dest_hbm,
+    hist_hbm,
     ev_hbm,
     ct_hbm,
     wu_hbm,
     wo_hbm,
-    event_grad_ref,
+    event_grad_hbm,
     layer_out_hbm,
     weight_grad_hbm,
+    dest_ref,
+    hist_ref,
     ev_ref,
     ct_all,
+    event_grad_ref,
     layer_out_ref,
     weight_grad_ref,
     wu,
@@ -148,7 +151,11 @@
     load_ct = pltpu.make_async_copy(ct_hbm, ct_ref, load_sem.at[3])
     load_wu = pltpu.make_async_copy(wu_hbm, wu, load_sem.at[0])
     load_wo = pltpu.make_async_copy(wo_hbm, wo, load_sem.at[1])
+    load_dest = pltpu.make_async_copy(dest_hbm, dest_ref, load_sem.at[4])
+    load_hist = pltpu.make_async_copy(hist_hbm, hist_ref, load_sem.at[5])
+    load_dest.start()
     load_ev.start()
+    load_hist.start()
 
     barrier = pltpu.get_barrier_semaphore()
 
@@ -171,6 +178,7 @@
     ri = iota((rows, rows), 0)
     ci = iota((rows, rows), 1)
     eye = ri == ci
+    load_dest.wait()
     d_row = jnp.broadcast_to(dest_ref[...], (rows, rows))
     d_col = jnp.sum(jnp.where(eye, d_row.astype(F32), 0.0), axis=1, keepdims=True)
     d_col = jnp.broadcast_to(d_col, (rows, rows)).astype(I32)
@@ -225,6 +233,7 @@
 
     lax.fori_loop(1, n_dp, to_group(ev_send, ev_recv, ev_sems, block), 0)
 
+    load_hist.wait()
     for b in range(n_chain):
         ids = jnp.broadcast_to(
             hist_ref[:, rows * b : rows * (b + 1)].astype(F32), (rows, rows)
@@ -588,17 +597,6 @@
         chain_copy(full_send, full_recv.at[c], full_ss, full_rs, peer).start()
     full_recv[c] = full_send[...]
 
-    await_group(ret_recv, ret_sems.at[1], block)
-    returned = ret_recv[...]
-    for q in range(fold):
-        event_grad_ref[:, cols * q : cols * (q + 1)] = dot(home_ref[q], returned).astype(BF)
-
-    await_chain(full_send, full_recv.at[0], full_ss, full_rs)
-    for h in range(n_chain):
-        weight_grad_ref[:, h * head : (h + 1) * head] = full_recv[h].astype(F32)
-    store_wg = pltpu.make_async_copy(weight_grad_ref, weight_grad_hbm, store_sem.at[1])
-    store_wg.start()
-
     await_group(ev_send, ev_sems.at[0], block)
     await_group(ct_all, ct_sems.at[0], rows, team - 1)
     await_group(gt_recv, gt_sems.at[0], rows, team - 1)
@@ -607,15 +605,30 @@
         def _(k=k):
             pltpu.make_async_copy(wg_send.at[k], wg_send.at[k], wg_ss.at[k]).wait()
 
-    await_group(ret_send, ret_sems.at[0], block)
     await_sent(qkv_send.at[0], qkv.at[pl.ds(0, rows)], qkv_ss, qkv_rs)
     await_sent(mix_send.at[pl.ds(0, rows)], mix_recv.at[0], mix_ss, mix_rs)
     await_sent(h_send.at[0], h_recv.at[pl.ds(0, rows)], h_ss, h_rs)
     await_sent(stat_send, stat_recv.at[0], stat_ss, stat_rs)
     await_sent(d_send.at[0], d_recv.at[0], d_ss, d_rs)
     await_sent(part_send.at[0], part_recv.at[0], part_ss, part_rs)
+    store_lo.wait()
+
+    await_group(ret_recv, ret_sems.at[1], block)
+    returned = ret_recv[...]
+    for q in range(fold):
+        event_grad_ref[:, cols * q : cols * (q + 1)] = dot(home_ref[q], returned).astype(BF)
+    store_eg = pltpu.make_async_copy(event_grad_ref, event_grad_hbm, store_sem.at[2])
+    store_eg.start()
+
+    await_chain(full_send, full_recv.at[0], full_ss, full_rs)
+    for h in range(n_chain):
+        weight_grad_ref[:, h * head : (h + 1) * head] = full_recv[h].astype(F32)
+    store_wg = pltpu.make_async_copy(weight_grad_ref, weight_grad_hbm, store_sem.at[1])
+    store_wg.start()
+
+    await_group(ret_send, ret_sems.at[0], block)
     await_sent(full_send, full_recv.at[0], full_ss, full_rs)
-    store_lo.wait()
+    store_eg.wait()
     store_wg.wait()
 
 
@@ -646,11 +659,14 @@
             jax.ShapeDtypeStruct((rows, width), BF),
             jax.ShapeDtypeStruct((share, width), F32),
         ),
-        in_specs=[vmem, vmem, anywhere, anywhere, anywhere, anywhere],
-        out_specs=(vmem, anywhere, anywhere),
+        in_specs=[anywhere, anywhere, anywhere, anywhere, anywhere, anywhere],
+        out_specs=(anywhere, anywhere, anywhere),
         scratch_shapes=[
+            pltpu.VMEM((1, rows), I32),
+            pltpu.VMEM((1, tokens), I32),
             pltpu.VMEM((rows, width), BF),
             pltpu.VMEM((width, width), BF),
+            pltpu.VMEM((rows, width), BF),
             pltpu.VMEM((rows, width), BF),
             pltpu.VMEM((share, width), F32),
             pltpu.VMEM((width, 4 * width), BF),
@@ -697,8 +713,8 @@
             pltpu.VMEM((rows, rows), F32),
             pltpu.VMEM((total, cols), BF),
             pltpu.VMEM((total, cols), BF),
-            pltpu.SemaphoreType.DMA((4,)),
-            pair,
+            pltpu.SemaphoreType.DMA((6,)),
+            pltpu.SemaphoreType.DMA((3,)),
             pair,
             pair,
             pair,

time: 85.6 us -> 84.5 us (0.987)
  Pallas kernels: 84.8 us -> 83.7 us
    pallas_call x1, Pallas kernels: 82.9 us -> 81.8 us  [on_device(): pl.pallas_call(functools.partial(kernel, n_dp, n_chain), out_shape=(jax.S...]
where the time goes in v4:
time: 84.5 us; the launch traced here: 84.4 us
  Pallas kernels  83.7 us (99%)
    pallas_call x1, Pallas kernels, on_device(): pl.pallas_call(functools.partial(kernel, n_dp, n_chain), out_shape=(jax.S...  81.8 us
    pallas_call x1, Pallas kernels, on_device(): pl.pallas_call(hand_over, out_shape=tuple((jax.ShapeDtypeStruct(r.shape,...  1.91 us

profile of v4, /device:TPU:1, one launch (start us, length us, event | category | flops | bytes accessed | tf_op | source)
XLA Modules:
  0.0 84.4 jit_solution(498622607076923165)
XLA Ops:
  0.6 81.8 %hstu_layer.1 = (bf16[128,1024]{1,0:T(8,128)(2,1)}, bf16[128,1024]{1,0:T(8,128)(2,1)}, f32[32,1024]{1,0:T(8,128)}) custom-call(s32[1,128]{1,0:T(1,128)} %dest_hbm.1, s32[1,1024]{1,0:T(1,128)} %hist_hbm.1, bf16[128,1024]{1,0:T(8,128)(2,1)} %bitcast.4, bf16[128,1024]{1,0:T(8,128)(2,1)} %bitcast.5, bf16[1024,4096]{1,0:T(8,128)(2,1)} %wu_hbm.1, ...), custom_call_target="tpu_custom_call" | custom-call | flops 9663676416 | bytes 12582912 | tf_op jit(solution)/shard_map/hstu_layer/pallas_call | solution.py:655
  82.5 1.9 %hand_over.1 = (bf16[128,1024]{1,0:T(8,128)(2,1)}, bf16[128,1024]{1,0:T(8,128)(2,1)}, f32[32,1024]{1,0:T(8,128)}) custom-call(bf16[128,1024]{1,0:T(8,128)(2,1)} %get-tuple-element.9.a, bf16[128,1024]{1,0:T(8,128)(2,1)} %get-tuple-element.10.b, f32[32,1024]{1,0:T(8,128)} %get-tuple-element.11.c), custom_call_target="tpu_custom_call" | custom-call | tf_op jit(solution)/shard_map/hand_over/pallas_call | solution.py:734

commit v5 on v4

--- a/solution.py
+++ b/solution.py
@@ -322,13 +322,13 @@
     gated_grad = dot_nt(ct_ref[...], wo[...])
     gated_grad_ref[...] = gated_grad
     upstream = gated_grad * gating_ref[...].astype(F32)
-    upstream = (upstream - mean(upstream)).astype(BF)
+    upstream = upstream - mean(upstream)
     for h in range(HEADS):
-        h_send[h] = upstream[:, h * head : (h + 1) * head]
+        h_send[h] = upstream[:, h * head : (h + 1) * head].T.astype(BF)
     for away in (4, 3, 5, 2, 6, 1, 7):
         peer = lax.rem(c + away, n_chain)
-        chain_copy(h_send.at[peer], h_recv.at[mine], h_ss, h_rs, peer).start()
-    h_recv[mine, :] = h_send[c]
+        chain_copy(h_send.at[peer], h_recv.at[c], h_ss, h_rs, peer).start()
+    h_recv[c] = h_send[c]
     to_team(lambda other: ct_ref, ct_ref, ct_sems)
 
     def to_slope(step, carry):
@@ -390,9 +390,9 @@
             )
         mix_t[:, at_i] = dot(value_t[:, until], att[until, at_i])
 
-    await_chain(h_send.at[0], h_recv.at[pl.ds(0, rows)], h_ss, h_rs)
+    await_chain(h_send.at[0], h_recv.at[0], h_ss, h_rs)
     mixed = mix_t[...]
-    upstream = h_recv[...].astype(F32).T
+    upstream = jnp.concatenate([h_recv[k] for k in range(n_chain)], axis=1).astype(F32)
     own_mean = jnp.mean(mixed, axis=0, keepdims=True)
     center = mixed - own_mean
     half = tokens // 2
@@ -607,7 +607,7 @@
 
     await_sent(qkv_send.at[0], qkv.at[pl.ds(0, rows)], qkv_ss, qkv_rs)
     await_sent(mix_send.at[pl.ds(0, rows)], mix_recv.at[0], mix_ss, mix_rs)
-    await_sent(h_send.at[0], h_recv.at[pl.ds(0, rows)], h_ss, h_rs)
+    await_sent(h_send.at[0], h_recv.at[0], h_ss, h_rs)
     await_sent(stat_send, stat_recv.at[0], stat_ss, stat_rs)
     await_sent(d_send.at[0], d_recv.at[0], d_ss, d_rs)
     await_sent(part_send.at[0], part_recv.at[0], part_ss, part_rs)
@@ -686,8 +686,8 @@
             pltpu.VMEM((tokens, tokens), BF),
             pltpu.VMEM((tokens, head), BF),
             pltpu.VMEM((n_chain, rows, head), BF),
-            pltpu.VMEM((n_chain, rows, head), BF),
-            pltpu.VMEM((tokens, head), BF),
+            pltpu.VMEM((n_chain, head, rows), BF),
+            pltpu.VMEM((n_chain, head, rows), BF),
             pltpu.VMEM((8, tokens // 2), F32),
             pltpu.VMEM((n_chain, 8, tokens // 2), F32),
             pltpu.VMEM((head, tokens), F32),

time: 84.5 us -> 84.2 us (level)
  no operation moved by 1% of the time
where the time goes in v5:
time: 84.2 us; the launch traced here: 84 us
  Pallas kernels  83.4 us (99%)
    pallas_call x1, Pallas kernels, on_device(): pl.pallas_call(functools.partial(kernel, n_dp, n_chain), out_shape=(jax.S...  81.5 us
    pallas_call x1, Pallas kernels, on_device(): pl.pallas_call(hand_over, out_shape=tuple((jax.ShapeDtypeStruct(r.shape,...  1.91 us

profile of v5, /device:TPU:1, one launch (start us, length us, event | category | flops | bytes accessed | tf_op | source)
XLA Modules:
  0.0 84.0 jit_solution(15750466610371648839)
XLA Ops:
  0.6 81.5 %hstu_layer.1 = (bf16[128,1024]{1,0:T(8,128)(2,1)}, bf16[128,1024]{1,0:T(8,128)(2,1)}, f32[32,1024]{1,0:T(8,128)}) custom-call(s32[1,128]{1,0:T(1,128)} %dest_hbm.1, s32[1,1024]{1,0:T(1,128)} %hist_hbm.1, bf16[128,1024]{1,0:T(8,128)(2,1)} %bitcast.4, bf16[128,1024]{1,0:T(8,128)(2,1)} %bitcast.5, bf16[1024,4096]{1,0:T(8,128)(2,1)} %wu_hbm.1, ...), custom_call_target="tpu_custom_call" | custom-call | flops 9663676416 | bytes 12582912 | tf_op jit(solution)/shard_map/hstu_layer/pallas_call | solution.py:655
  82.1 1.9 %hand_over.1 = (bf16[128,1024]{1,0:T(8,128)(2,1)}, bf16[128,1024]{1,0:T(8,128)(2,1)}, f32[32,1024]{1,0:T(8,128)}) custom-call(bf16[128,1024]{1,0:T(8,128)(2,1)} %get-tuple-element.9.a, bf16[128,1024]{1,0:T(8,128)(2,1)} %get-tuple-element.10.b, f32[32,1024]{1,0:T(8,128)} %get-tuple-element.11.c), custom_call_target="tpu_custom_call" | custom-call | tf_op jit(solution)/shard_map/hand_over/pallas_call | solution.py:734
